TPU v7x, 32 devices: a whole 2x2x4 slice. The times are simulated.
32 devices in a mesh: dp: 8 (over z, y), tensor: 4 (over x, core).
Axes of the slice: x: 2, y: 2, z: 4, core: 2. Of those that a mesh axis runs over, the one named last changes fastest.
Arguments:
- hidden_in: bfloat16 [32, 1024, 480], P('dp', 'tensor'), may hold values from -6 to 6
- attn_gain: float32 [480], replicated, may hold values from 0.25 to 1.75
- attn_shift: float32 [480], replicated, may hold values from -1.75 to 1.75
- query_key_value_weight: bfloat16 [3, 480, 480], P(None, None, 'tensor'), may hold values from -0.25 to 0.25
- query_key_value_bias: float32 [3, 480], P(None, 'tensor'), may hold values from -1.75 to 1.75
- attention_output_weight: bfloat16 [480, 480], P('tensor'), may hold values from -3.5 to 3.5
- out_bias: float32 [480], replicated, may hold values from -1.75 to 1.75
- ffn_gain: float32 [480], replicated, may hold values from 0.25 to 1.75
- ffn_shift: float32 [480], replicated, may hold values from -1.75 to 1.75
- up_projection_weight: bfloat16 [480, 1920], P('tensor', 'dp'), may hold values from -0.25 to 0.25
- up_projection_bias: float32 [1920], replicated, may hold values from -3 to 3
- down_projection_weight: bfloat16 [1920, 480], P('dp', 'tensor'), may hold values from -0.125 to 0.125
- down_bias: float32 [480], replicated, may hold values from -1.75 to 1.75
- lengths: int32 [32], P('dp'), may hold values from 204 to 1024, as said below
- cotangent: bfloat16 [32, 1024, 480], P('dp', 'tensor'), may hold values from -6 to 6
Outputs:
- hidden_out: bfloat16 [32, 1024, 480], P('dp', 'tensor')
- grad_hidden: bfloat16 [32, 1024, 480], P('dp', 'tensor')
- grad_attn_gain: float32 [480], replicated
- grad_attn_shift: float32 [480], replicated
- grad_qkv_weight: float32 [3, 480, 480], P(None, None, 'tensor')
- grad_qkv_bias: float32 [3, 480], P(None, 'tensor')
- grad_out_weight: float32 [480, 480], P('tensor')
- grad_out_bias: float32 [480], replicated
- grad_ffn_gain: float32 [480], replicated
- grad_ffn_shift: float32 [480], replicated
- grad_up_weight: float32 [480, 1920], P('tensor', 'dp')
- grad_up_bias: float32 [1920], replicated
- grad_down_weight: float32 [1920, 480], P('dp', 'tensor')
- grad_down_bias: float32 [480], replicated
Inputs may be any that keep to these rules, and one draw needn't show every extreme that they name: `lengths`: every index of dp holds at least one row longer than 768, and some row has exactly 1024.
All inputs are finite; a program needn't handle non-finite values.
Results may differ from a plain program's by a relative error of at most 0.012.
Values may be sent and summed in bfloat16 or wider, within the bound.
No kernel may reach another device: no remote copies, remote signals or barrier semaphores. Data moves between devices by JAX's collectives and lax.ppermute only.
A program may use at most 192 MiB of HBM per device.

v0:
```python
import math

import jax
import jax.numpy as jnp
import numpy as np
from jax import lax
from jax.experimental import pallas as pl
from jax.experimental.pallas import tpu as pltpu
from jax.sharding import PartitionSpec as P

HEAD_DIM = 24
HEAD_ROWS = 32
EPS = 1e-05
MASK_FILL = -1000000000.0
LOG2E = math.log2(math.e)
SAFE_SCORE = 58.0
WORK_SCALE = 0.01
BLOCK = 256
KEY_STEP = 256
LANES = 512
BF16 = jnp.bfloat16
F32 = jnp.float32

NN = (((1,), (0,)), ((), ()))
NT = (((1,), (1,)), ((), ()))
TN = (((0,), (0,)), ((), ()))


def product(left, right, dims=NN):
    return lax.dot_general(left, right, dims, preferred_element_type=F32)


def vmem(count):
    return [pl.BlockSpec(memory_space=pltpu.VMEM)] * count


def smem():
    return pl.BlockSpec(memory_space=pltpu.SMEM)


def hbm(count=1):
    return [pl.BlockSpec(memory_space=pltpu.HBM)] * count


def call(kernel, inputs, outs, scratch=(), in_specs=None, out_specs=None, limit=40, tiles=0):
    flops = int(2 * 256**3 * tiles * WORK_SCALE)
    in_specs = vmem(len(inputs)) if in_specs is None else in_specs
    inputs = [
        pltpu.with_memory_space_constraint(part, pltpu.HBM)
        if spec.memory_space is pltpu.HBM
        else part
        for part, spec in zip(inputs, in_specs)
    ]
    out_specs = vmem(len(outs)) if out_specs is None else out_specs
    outs = [
        pltpu.HBM(part.shape, part.dtype) if spec.memory_space is pltpu.HBM else part
        for part, spec in zip(outs, out_specs)
    ]
    return pl.pallas_call(
        kernel,
        out_shape=outs,
        in_specs=in_specs,
        out_specs=out_specs,
        scratch_shapes=list(scratch),
        compiler_params=pltpu.CompilerParams(vmem_limit_bytes=limit << 20),
        cost_estimate=pl.CostEstimate(flops=flops, transcendentals=0, bytes_accessed=0),
    )(*inputs)


def shape(dims, dtype):
    return jax.ShapeDtypeStruct(dims, dtype)


def at_block(index, size):
    return pl.ds(pl.multiple_of(index * size, size), size)


def split_three(values):
    high = values.astype(BF16).astype(F32)
    rest = values - high
    middle = rest.astype(BF16).astype(F32)
    return high, middle, rest - middle


def row_of(lengths, slot, rows):
    slot = jnp.where(slot == 0, 0, jnp.where(slot == 1, rows - 1, slot - 1))
    chosen = jnp.int32(0)
    for i in range(rows):
        rank = jnp.int32(0)
        for j in range(rows):
            if j < i:
                rank += jnp.where(lengths[j] <= lengths[i], 1, 0)
            elif j > i:
                rank += jnp.where(lengths[j] < lengths[i], 1, 0)
        chosen += jnp.where(rank == slot, i, 0)
    return chosen


def after(values, *others):
    return lax.optimization_barrier((values, *others))[0]


def norm_columns(values):
    centre = values - jnp.mean(values, axis=0, keepdims=True)
    inverse = lax.rsqrt(jnp.mean(centre * centre, axis=0, keepdims=True) + EPS)
    return centre * inverse, inverse


def norm_columns_back(upstream, unit, inverse, gain):
    scaled = upstream * gain
    centred = scaled - jnp.mean(scaled, axis=0, keepdims=True)
    return inverse * (centred - unit * jnp.mean(scaled * unit, axis=0, keepdims=True))


def pair_kernel(info, up, down, pair, up_inside, down_inside, semaphores):
    copies = [
        pltpu.make_async_copy(up, up_inside, semaphores.at[0]),
        pltpu.make_async_copy(down, down_inside, semaphores.at[1]),
    ]
    for copy in copies:
        copy.start()
    pair[...] = jnp.zeros_like(pair)
    for copy in copies:
        copy.wait()
    size = up.shape[1]
    up_half = up_inside[...]
    down_half = down_inside[...].astype(F32).T.astype(BF16)

    @pl.when(info[0] & 1 == 0)
    def _():
        pair[:, :size] = up_half
        pair[:, BLOCK : BLOCK + size] = down_half

    @pl.when(info[0] & 1 == 1)
    def _():
        pair[:, :size] = down_half
        pair[:, BLOCK : BLOCK + size] = up_half


def norm_kernel(
    lengths,
    hidden_in,
    gain,
    shift,
    out_weight_in,
    first_out,
    second_out,
    hidden,
    gain_inside,
    shift_inside,
    out_weight,
    rows_scratch,
    semaphores,
):
    rows, width, chunk = hidden.shape
    copies = [
        pltpu.make_async_copy(
            hidden_in.at[row_of(lengths, slot, rows)], hidden.at[slot], semaphores.at[slot]
        )
        for slot in range(rows)
    ]
    others = [
        pltpu.make_async_copy(gain, gain_inside, semaphores.at[4]),
        pltpu.make_async_copy(shift, shift_inside, semaphores.at[5]),
        pltpu.make_async_copy(out_weight_in, out_weight, semaphores.at[6]),
    ]
    for copy in others[:2] + copies + others[2:]:
        copy.start()
    rows_scratch[...] = jnp.zeros_like(rows_scratch)
    others[0].wait()
    others[1].wait()
    rows_scratch[0:1, :] = gain_inside[...]
    rows_scratch[1:2, :] = shift_inside[...]
    columns = rows_scratch[...].T
    half = rows // 2
    for row in range(rows):
        copies[row].wait()
        unit, _ = norm_columns(hidden[row].astype(F32))
        target = first_out if row < half else second_out
        place = row % half * width
        target[place : place + width, :] = (unit * columns[:, 0:1] + columns[:, 1:2]).astype(
            BF16
        )
    others[2].wait()
    own = out_weight.shape[0]
    second_out[half * width : half * width + own, :] = out_weight[:, :chunk]
    rest = width - chunk
    second_out[half * width + own : half * width + 2 * own, :] = jnp.zeros((own, chunk), BF16)
    second_out[half * width + own : half * width + 2 * own, :rest] = out_weight[:, chunk:]


def prepare_kernel(heads, info, *refs):
    outside, refs = refs[:9], refs[9:]
    weight_out, weight_turned_out, columns_out, bias_out, up_bias_out, vector_rows = refs[:6]
    weight_scratch, bias_rows = refs[6:8]
    inside, semaphores = refs[8:17], refs[17]
    copies = [
        pltpu.make_async_copy(source, target, semaphores.at[place])
        for place, (source, target) in enumerate(zip(outside, inside))
    ]
    for copy in copies:
        copy.start()
    vectors, (up_bias, weight, bias) = inside[:6], inside[6:]
    width = weight.shape[1]
    vector_rows[...] = jnp.zeros_like(vector_rows)
    for copy in copies:
        copy.wait()
    for place, vector in enumerate(vectors):
        vector_rows[place : place + 1, :] = vector[...]
    columns_out[...] = jnp.concatenate([vector_rows[...], jnp.zeros((120, width), F32)]).T
    span = heads * HEAD_DIM
    for c in range(3):
        own = slice(c * span, (c + 1) * span)
        weight_scratch[own, :] = weight[c].astype(F32).T
        bias_out[own, :] = jnp.broadcast_to(bias[c : c + 1, :], (128, span)).T
    weight_out[...] = weight_scratch[...].astype(BF16)
    weight_turned_out[...] = weight_scratch[...].T.astype(BF16)
    bias_rows[...] = jnp.zeros_like(bias_rows)
    count = up_bias.shape[1]
    block = count // 8
    spread = jnp.broadcast_to(up_bias[...], (8, count))
    for j in range(8):
        moved = pltpu.roll(spread, lax.rem(count - (info[1] ^ j) * block, count), 1)
        bias_rows[j : j + 1, :block] = moved[0:1, :block]
    up_bias_out[...] = bias_rows[...].T


def assemble_kernel(chunks, info, *refs):
    parts, (out, rows) = refs[:chunks], refs[chunks:]
    size = parts[0].shape[0]
    for k in range(chunks):
        half = parts[k][:, (k & 1) * BLOCK : ((k & 1) + 1) * BLOCK]
        rows[at_block(info[0] ^ k, size), :] = half.astype(F32)
    out[...] = rows[...].astype(BF16)


def rotary_constants(chunk, chunks):
    half = HEAD_DIM // 2
    element = np.arange(HEAD_DIM)
    frequency = (1.0 / 10000.0 ** (np.arange(0, HEAD_DIM, 2).astype(np.float32) / HEAD_DIM)).astype(
        np.float32
    )
    per_row = frequency[element % half].astype(np.float64)
    inner = per_row[:, None] * np.arange(chunk)[None, :]
    outer = per_row[:, None] * (np.arange(chunks) * chunk)[None, :]
    outer = np.repeat(outer[:, :, None], chunk, axis=2).transpose(1, 0, 2)
    inner_pair = np.stack([np.cos(inner), np.sin(inner)]).astype(np.float32)
    outer_pair = np.stack([np.cos(outer), np.sin(outer)]).astype(np.float32)
    return inner_pair, outer_pair


def chunk_tables(inner, outer, index):
    cos_in, sin_in = inner[0], inner[1]
    cos_out, sin_out = outer[0, index], outer[1, index]
    element = lax.broadcasted_iota(jnp.int32, cos_in.shape, 0)
    sine = sin_in * cos_out + cos_in * sin_out
    return cos_in * cos_out - sin_in * sin_out, jnp.where(
        element < HEAD_DIM // 2, -sine, sine
    )


def swap_halves(values):
    return pltpu.roll(values, HEAD_DIM // 2, 0)


def attend_kernel(heads, chunks, chunk, first_row, rows, info, lengths, *refs):
    parts = refs[:chunks]
    weight, bias, inner, outer, own_out, near_out, cross_out = refs[chunks : chunks + 7]
    queries, keys, values, logsum, mixed_turned, normed_out, key_rows, peak, flat = refs[
        chunks + 7 : chunks + 16
    ]
    normed, semaphores = refs[chunks + 16 :]
    position = info[0]
    width = normed.shape[1]
    full = chunk * chunks
    span = heads * HEAD_DIM
    scale = HEAD_DIM**-0.5

    def one_row(r, carry):
        length = lengths[row_of(lengths, first_row + r, lengths.shape[0])]
        for k in range(chunks):
            normed[r, :, at_block(position ^ k, chunk)] = parts[k][at_block(r, width), :]
        pltpu.make_async_copy(normed.at[r], normed_out.at[r], semaphores.at[r]).start()
        flat[...] = product(weight[...], normed[r])
        line = lax.broadcasted_iota(jnp.int32, (8, chunk), 0)
        ones = jnp.where(line < 3, 1.0, 0.0)
        query_line = jnp.where(line == 3, 1.0, 0.0)
        query_top = [jnp.zeros((1, chunk), F32) for _ in range(heads)]
        key_top = [jnp.zeros((1, chunk), F32) for _ in range(heads)]
        for j in range(chunks):
            at = slice(j * chunk, (j + 1) * chunk)
            cosine, sine = chunk_tables(inner, outer, j)
            query_cosine, query_sine = cosine * scale, sine * scale
            place = lax.broadcasted_iota(jnp.int32, (8, chunk), 1) + j * chunk
            key_line = jnp.where((line == 3) & (place >= length), MASK_FILL, ones)
            for h in range(heads):
                here = h * HEAD_DIM
                query, key, value = (
                    flat[c * span + here : c * span + here + HEAD_DIM, at]
                    + jnp.concatenate(
                        [bias[c * span + here : c * span + here + HEAD_DIM, :]] * (chunk // 128),
                        axis=1,
                    )
                    for c in range(3)
                )
                query = query * query_cosine + swap_halves(query) * query_sine
                key = key * cosine + swap_halves(key) * sine
                query_top[h] = jnp.maximum(
                    query_top[h], jnp.sum(query * query, axis=0, keepdims=True)
                )
                key_top[h] = jnp.maximum(key_top[h], jnp.sum(key * key, axis=0, keepdims=True))
                key_full = jnp.concatenate([key, key_line])
                queries[r, h, :, at] = jnp.concatenate([query, query_line]).astype(BF16)
                keys[r, h, :, at] = key_full.astype(BF16)
                values[r, h, :, at] = jnp.concatenate([value, ones]).astype(BF16)
                key_rows[h, at, :] = key_full.T.astype(BF16)
        bound = jnp.zeros((1, 1), F32)
        for h in range(heads):
            bound = jnp.maximum(
                bound,
                jnp.max(query_top[h], axis=-1, keepdims=True)
                * jnp.max(key_top[h], axis=-1, keepdims=True),
            )
        safe = jnp.max(bound) <= SAFE_SCORE * SAFE_SCORE
        peak[...] = jnp.zeros_like(peak)

        @pl.when(jnp.logical_not(safe))
        def _():
            def one_head(h, carry):
                scores = product(key_rows[h], queries[r, h])
                peak[pl.ds(h, 1), :] = (
                    jnp.max(scores, axis=0, keepdims=True).astype(BF16).astype(F32)
                )
                return carry

            lax.fori_loop(0, heads, one_head, 0)

        head_line = lax.broadcasted_iota(jnp.int32, (HEAD_ROWS, full), 0)

        def with_keys(count):
            def one_head(h, carry):
                top = peak[pl.ds(h, 1), :]
                query = jnp.where(
                    head_line == HEAD_DIM, -top, queries[r, h].astype(F32)
                ).astype(BF16)
                exponent = jnp.exp(product(key_rows[h, :count, :], query)).astype(BF16)
                blend = product(values[r, h, :, :count], exponent)
                total = blend[HEAD_DIM : HEAD_DIM + 1, :]
                logsum[r, pl.ds(h, 1), :] = top + jnp.log(total)
                mixed_turned[r, pl.ds(pl.multiple_of(h * HEAD_DIM, 8), HEAD_DIM), :] = blend[
                    :HEAD_DIM
                ] * (1.0 / total)
                return carry

            lax.fori_loop(0, heads, one_head, 0, unroll=True)

        blocks = jnp.maximum((length + KEY_STEP - 1) // KEY_STEP, 1)
        for b in range(1, full // KEY_STEP + 1):
            pl.when(blocks == b)(lambda b=b: with_keys(b * KEY_STEP))
        mixed_turned[r, span:, :] = jnp.zeros((mixed_turned.shape[1] - span, full), F32)
        own_out[r] = mixed_turned[r, :, at_block(position, chunk)].astype(BF16)
        near_out[r] = mixed_turned[r, :, at_block(position ^ 1, chunk)].astype(BF16)
        cross_out[r, 0] = mixed_turned[r, :, at_block(position ^ 2, chunk)].astype(BF16)
        cross_out[r, 1] = mixed_turned[r, :, at_block(position ^ 3, chunk)].astype(BF16)
        return carry

    lax.fori_loop(0, rows, one_row, 0)
    for r in range(rows):
        pltpu.make_async_copy(normed.at[r], normed_out.at[r], semaphores.at[r]).wait()


def attend_back_kernel(heads, chunks, chunk, row, local, first, last, info, lengths, *refs):
    upstream_own, upstream_near, upstream_cross, upstream_far = refs[:4]
    queries, keys, values, logsum, mixed_turned, normed_in, weight_turned, inner, outer = refs[
        4:13
    ]
    refs = refs[13:]
    if not first:
        carried = refs[0]
        refs = refs[1:]
    if last:
        out_own, out_near, out_cross, weight, vector_rows = refs[:5]
        refs = refs[5:]
    own_out, near_out, cross_out = refs[:3]
    refs = refs[3:]
    if last:
        even_pieces, odd_pieces, norm_sums = refs[:3]
        refs = refs[3:]
    else:
        running = refs[0]
        refs = refs[1:]
    (
        upstream,
        query_full,
        upstream_full,
        key_rows,
        value_rows,
        grads,
        grad_low,
        packed,
        normed,
        semaphore,
    ) = refs
    fetch = pltpu.make_async_copy(normed_in.at[local], normed, semaphore)
    fetch.start()
    position, index = info[0], info[1]
    length = lengths[row_of(lengths, row, lengths.shape[0])]
    full = chunk * chunks
    span = heads * HEAD_DIM
    upstream[:, at_block(position, chunk)] = upstream_own[local]
    upstream[:, at_block(position ^ 1, chunk)] = upstream_near[local]
    upstream[:, at_block(position ^ 2, chunk)] = upstream_cross[local, 0]
    upstream[:, at_block(position ^ 3, chunk)] = upstream_far[local, 1]
    zeros = jnp.zeros((5, chunk), F32)
    line = lax.broadcasted_iota(jnp.int32, (8, chunk), 0)
    for j in range(chunks):
        at = slice(j * chunk, (j + 1) * chunk)
        turned = upstream[:, at].astype(F32)
        blend = turned * mixed_turned[local, :, at]
        for h in range(heads):
            own = slice(h * HEAD_DIM, (h + 1) * HEAD_DIM)
            high, middle, rest = split_three(-jnp.sum(blend[own], axis=0, keepdims=True))
            extra = jnp.where(
                line == 0, high, jnp.where(line == 1, middle, jnp.where(line == 2, rest, 0.0))
            )
            upstream_full[h, :, at] = jnp.concatenate([turned[own], extra]).astype(BF16)
            high, middle, rest = split_three(-logsum[local, h : h + 1, at])
            extra = jnp.where(
                line == 0,
                high,
                jnp.where(
                    line == 1, middle, jnp.where(line == 2, rest, jnp.where(line == 3, 1.0, 0.0))
                ),
            )
            query = queries[local, h, :, at].astype(F32)[:HEAD_DIM]
            query_full[h, :, at] = jnp.concatenate([query, extra]).astype(BF16)
            key_rows[h, at, :] = keys[local, h, :, at].astype(F32).T.astype(BF16)
            value_rows[h, at, :] = values[local, h, :, at].astype(F32).T.astype(BF16)

    def with_keys(count):
        def one_head(h, carry):
            own = pl.ds(pl.multiple_of(h * HEAD_DIM, 8), HEAD_DIM)
            grad_query = jnp.zeros((HEAD_ROWS, full), F32)
            for place in range(0, count, BLOCK):
                at = slice(place, min(place + BLOCK, count))
                probs = jnp.exp(product(key_rows[h, at, :], query_full[h])).astype(BF16)
                grad_probs = product(value_rows[h, at, :], upstream_full[h]).astype(BF16)
                grad_scores = probs * grad_probs
                grads[2, own, at] = product(upstream_full[h], probs, NT)[:HEAD_DIM]
                grads[1, own, at] = product(query_full[h], grad_scores, NT)[:HEAD_DIM]
                grad_query += product(keys[local, h, :, at], grad_scores)
            grads[0, own, :] = grad_query[:HEAD_DIM]
            return carry

        lax.fori_loop(0, heads, one_head, 0)
        if count < full:
            grads[1, :, count:] = jnp.zeros((span, full - count), F32)
            grads[2, :, count:] = jnp.zeros((span, full - count), F32)

    blocks = jnp.maximum((length + KEY_STEP - 1) // KEY_STEP, 1)
    for b in range(1, full // KEY_STEP + 1):
        pl.when(blocks == b)(lambda b=b: with_keys(b * KEY_STEP))

    sums = [[jnp.zeros((HEAD_DIM, 128), F32) for _ in range(heads)] for _ in range(3)]
    for j in range(chunks):
        at = slice(j * chunk, (j + 1) * chunk)
        cosine, sine = chunk_tables(inner, outer, j)
        query_cosine, query_sine = cosine * HEAD_DIM**-0.5, sine * HEAD_DIM**-0.5
        for h in range(heads):
            own = slice(h * HEAD_DIM, (h + 1) * HEAD_DIM)
            query, key, value = (grads[c, own, at] for c in range(3))
            query = query * query_cosine - swap_halves(query) * query_sine
            key = key * cosine - swap_halves(key) * sine
            for c, part in enumerate((query, key, value)):
                for piece in range(chunk // 128):
                    sums[c][h] = sums[c][h] + part[:, piece * 128 : (piece + 1) * 128]
                grads[c, own, at] = part
    for c in range(3):
        grad_low[c * span : (c + 1) * span, :] = grads[c].astype(BF16)
    for k in range(chunks):
        result = product(
            weight_turned[...], grad_low[:, at_block(position ^ k, chunk)]
        ).astype(BF16)
        if k == 0:
            own_out[...] = result
        elif k == 2:
            cross_out[...] = result
        else:
            near_out[k // 2] = result
    width = weight_turned.shape[0]
    fetch.wait()
    result = product(grad_low[...], normed[...], NT)
    bias_grad = jnp.concatenate(
        [jnp.sum(part, axis=1, keepdims=True) for group in sums for part in group]
    )
    bias_grad = jnp.broadcast_to(bias_grad, (3 * span, 128))
    if not first:
        result = result + carried[:, :width]
        bias_grad = bias_grad + carried[:, LANES:]
    if not last:
        running[:, :width] = result
        running[:, LANES:] = bias_grad
        return
    packed[: 3 * span, :width] = result
    gain_sum = jnp.zeros((8, width), F32)
    shift_sum = jnp.zeros((8, width), F32)
    gain, shift = vector_rows[0:1, :], vector_rows[1:2, :]
    for place in range(0, 3 * span, 8):
        own = slice(place, place + 8)
        factor = weight[own, :].astype(F32)
        column = bias_grad[own, 0:1]
        gain_sum = gain_sum + factor * (result[own] - shift * column)
        shift_sum = shift_sum + factor * column
    norm_sums[...] = jnp.zeros_like(norm_sums)
    norm_sums[0:1, :] = jnp.sum(gain_sum, axis=0, keepdims=True) / gain
    norm_sums[1:2, :] = jnp.sum(shift_sum, axis=0, keepdims=True)
    lane = lax.broadcasted_iota(jnp.int32, (3 * span, 128), 1)
    packed[: 3 * span, LANES - 128 :] = jnp.where(
        lane >= width - (LANES - 128), bias_grad, packed[: 3 * span, LANES - 128 :]
    )
    shared = (out_own[...].astype(F32) + out_near[0].astype(F32)) + out_cross[...].astype(F32)
    packed[3 * span : 4 * span, :] = shared[:span]
    packed[4 * span : 4 * span + 16, :] = shared[128:144]
    packed[4 * span + 16 :, :] = jnp.zeros((packed.shape[0] - 4 * span - 16, LANES), F32)
    size = packed.shape[0] // 8
    for j in range(8):
        target = odd_pieces if j % 2 else even_pieces
        target[j // 2] = packed[at_block(index ^ j, size), :].astype(BF16)


def gelu_parts(values):
    magnitude = jnp.abs(values) * (0.5**0.5)
    density = jnp.exp2(values * values * (-0.5 * LOG2E))
    divisor = 1.0 + 0.3275911 * magnitude
    step = pl.reciprocal(divisor, approx=True)
    step = step * (2.0 - divisor * step)
    series = 1.061405429 * step - 1.453152027
    series = series * step + 1.421413741
    series = series * step - 0.284496736
    series = series * step + 0.254829592
    tail = 0.5 * series * step * density
    share = jnp.where(values < 0, tail, 1.0 - tail)
    return share, density * (1.0 / math.sqrt(2.0 * math.pi))


def lane_groups(values):
    total = values[:, :128]
    for place in range(128, values.shape[1], 128):
        total = total + values[:, place : place + 128]
    return total


def row_sum(values):
    total = values[:8]
    for place in range(8, values.shape[0], 8):
        total = total + values[place : place + 8]
    return total


def feed_kernel(chunks, blocks, first_row, rows, last, info, lengths, *refs):
    hidden, cotangent, columns, up_bias = refs[:4]
    mixed_own, mixed_near, mixed_cross, mixed_far = refs[4:8]
    out_weight = refs[8 : 8 + chunks]
    refs = refs[8 + chunks :]
    if last:
        weights, carried, out_carried, sums_carried, bias_carried, hidden_before = refs[:6]
        refs = refs[6:]
    else:
        feeds, refs = refs[:12], refs[12:]
    hidden_out, grad_middle_out, grad_own, grad_near, grad_cross = refs[:5]
    refs = refs[5:]
    if last:
        kept_out, sent_out, out_own, out_near, out_cross = refs[:5]
    else:
        weights, carried, out_carried, sums_carried, bias_carried = refs[:5]
    refs = refs[5:]
    (
        out_rows,
        mixed,
        source,
        given,
        low_rows,
        down_total,
        back_total,
        upward,
        upstream,
        active,
        grad_low,
        sums_total,
        bias_total,
        shared,
        semaphores,
    ) = refs
    core, index = info[0] & 1, info[1]
    width, chunk = hidden.shape[1:]
    tokens = rows * chunk
    held = mixed_own.shape[1]
    places = [row_of(lengths, first_row + r, hidden.shape[0]) for r in range(rows)]
    if not last:
        copies = []
        for side in range(2):
            sources = list(feeds[6 * side : 6 * side + 4])
            duo, duo_beside = feeds[6 * side + 4 : 6 * side + 6]
            place = core if side == 0 else 1 - core
            for e in range(2):
                sources += [duo.at[e], duo_beside.at[e]]
            for j in range(blocks):
                copies.append(
                    pltpu.make_async_copy(
                        sources[j],
                        weights.at[place, :, j * BLOCK : (j + 1) * BLOCK],
                        semaphores.at[side, j],
                    )
                )
        for copy in copies:
            copy.start()
    own_rows = (out_weight[0].shape[0] - 2 * width) // 2
    for k in range(chunks):
        base = 2 * width
        at = k * held
        out_rows[at : at + held, :] = jnp.zeros((held, width), BF16)
        out_rows[at : at + own_rows, :chunk] = out_weight[k][base : base + own_rows, :]
        out_rows[at : at + own_rows, chunk:] = out_weight[k][
            base + own_rows : base + 2 * own_rows, : width - chunk
        ]
    for r in range(rows):
        at = slice(r * chunk, (r + 1) * chunk)
        mixed[0 * held : 1 * held, at] = mixed_own[r]
        mixed[1 * held : 2 * held, at] = mixed_near[r]
        mixed[2 * held : 3 * held, at] = mixed_cross[r, 0]
        mixed[3 * held : 4 * held, at] = mixed_far[r, 1]
        given[:, at] = cotangent[places[r]]
    source[...] = product(out_rows[...], mixed[...], TN)
    step = 32
    pieces = [slice(place, place + step) for place in range(0, width, step)]

    total = jnp.zeros((8, tokens), F32)
    for own in pieces:
        entered = jnp.concatenate([hidden[places[r], own, :] for r in range(rows)], axis=1)
        middle = source[own, :] + entered.astype(F32) + columns[own, 2:3]
        source[own, :] = middle
        total = total + row_sum(middle)
    mean = jnp.sum(total, axis=0, keepdims=True) * (1.0 / width)
    total = jnp.zeros((8, tokens), F32)
    for own in pieces:
        centre = source[own, :] - mean
        total = total + row_sum(centre * centre)
    inverse = lax.rsqrt(jnp.sum(total, axis=0, keepdims=True) * (1.0 / width) + EPS)
    for own in pieces:
        middle = source[own, :]
        unit = (middle - mean) * inverse
        low_rows[own, :] = (unit * columns[own, 3:4] + columns[own, 4:5]).astype(BF16)
        down_total[own, :] = middle + columns[own, 5:6]
        source[own, :] = unit
    back_total[...] = jnp.zeros_like(back_total)
    if not last:
        for copy in copies:
            copy.wait()

    pair = 2 * BLOCK

    def enter(i, slot):
        at = at_block(i, pair)
        upward[slot] = product(weights[0, :, at], low_rows[...], TN)
        upstream[slot] = product(weights[1, :, at], given[...], TN)

    lane = lax.broadcasted_iota(jnp.int32, (step, 128), 1)

    def bend(i, slot):
        for place in range(0, pair, step):
            own = slice(place, place + step)
            j = 2 * i + place // BLOCK
            inside = slice(place % BLOCK, place % BLOCK + step)
            bias = jnp.sum(
                jnp.where(lane == j, up_bias[inside, :], 0.0), axis=1, keepdims=True
            )
            values = upward[slot, own, :] + bias
            share, density = gelu_parts(values)
            active[slot, own, :] = (values * share).astype(BF16)
            grad_up = upstream[slot, own, :] * (share + values * density)
            grad_low[slot, own, :] = grad_up.astype(BF16)
            bias_sum = lane_groups(grad_up)
            if last:
                bias_total[j, inside, :] = bias_sum + bias_carried[j, inside, :]
            else:
                bias_carried[j, inside, :] = bias_sum

    def leave(i, slot):
        at = at_block(i, pair)
        down_total[...] += product(weights[1, :, at], active[slot])
        back_total[...] += product(weights[0, :, at], grad_low[slot])
        up_grad = product(low_rows[...], grad_low[slot], NT)
        down_grad = product(given[...], active[slot], NT)
        if not last:
            carried[0, :, at] = up_grad
            carried[1, :, at] = down_grad
            return
        up_grad = up_grad + carried[0, :, at]
        down_grad = down_grad + carried[1, :, at]
        kept = jnp.where(core == 0, up_grad, down_grad).astype(BF16)
        sent = jnp.where(core == 0, down_grad, up_grad).astype(BF16)
        for odd in range(2):
            kept_out[odd, i] = kept[:, odd * BLOCK : (odd + 1) * BLOCK]
            sent_out[odd, i] = sent[:, odd * BLOCK : (odd + 1) * BLOCK]

    def two_pairs(n, carry):
        i = 2 * n
        enter(i + 1, 1)
        bend(i, 0)
        leave(i, 0)
        enter(lax.rem(i + 2, blocks // 2), 0)
        bend(i + 1, 1)
        leave(i + 1, 1)
        return carry

    enter(0, 0)
    lax.fori_loop(0, blocks // 4, two_pairs, 0)
    if last:
        for r in range(first_row):
            hidden_out[row_of(lengths, r, hidden.shape[0])] = hidden_before[r]
    for r in range(rows):
        place = places[r] if last else r
        hidden_out[place] = down_total[:, r * chunk : (r + 1) * chunk].astype(BF16)
    scaled_total = jnp.zeros((8, tokens), F32)
    unit_total = jnp.zeros((8, tokens), F32)
    for own in pieces:
        scaled = back_total[own, :] * columns[own, 3:4]
        scaled_total = scaled_total + row_sum(scaled)
        unit_total = unit_total + row_sum(scaled * source[own, :])
    scaled_mean = jnp.sum(scaled_total, axis=0, keepdims=True) * (1.0 / width)
    unit_mean = jnp.sum(unit_total, axis=0, keepdims=True) * (1.0 / width)
    for own in pieces:
        back, unit = back_total[own, :], source[own, :]
        given_wide = given[own, :].astype(F32)
        scaled = back * columns[own, 3:4]
        grad_middle = given_wide + inverse * (scaled - scaled_mean - unit * unit_mean)
        for r in range(rows):
            grad_middle_out[r, own, :] = grad_middle[:, r * chunk : (r + 1) * chunk]
        low_rows[own, :] = grad_middle.astype(BF16)
        for place, part in enumerate((back * unit, back, grad_middle, given_wide)):
            part = lane_groups(part)
            if last:
                sums_total[place, own, :] = part + sums_carried[place, own, :]
            else:
                sums_carried[place, own, :] = part
    mixed_grad = product(out_rows[...], low_rows[...]).astype(BF16)
    for r in range(rows):
        at = slice(r * chunk, (r + 1) * chunk)
        grad_own[r] = mixed_grad[:held, at]
        grad_near[r] = mixed_grad[held : 2 * held, at]
        grad_cross[r, 0] = mixed_grad[2 * held : 3 * held, at]
        grad_cross[r, 1] = mixed_grad[3 * held :, at]
    out_part = product(mixed[...], low_rows[...], NT)
    if not last:
        out_carried[...] = out_part
        return
    out_part = (out_part + out_carried[...]).astype(BF16)
    shared[...] = jnp.zeros_like(shared)
    for place in range(4):
        line = row_sum(sums_total[place].T)
        shared[place : place + 1, :width] = jnp.sum(line, axis=0, keepdims=True)
    for j in range(blocks):
        line = row_sum(bias_total[j].T)
        shared[pl.ds(4 + (index ^ j), 1), :BLOCK] = jnp.sum(line, axis=0, keepdims=True)
    shared_low = shared[...].astype(BF16)
    for k, target in enumerate((out_own, out_near.at[0], out_cross, out_near.at[1])):
        target[:held, 384:] = jnp.zeros((held, LANES - 384), BF16)
        target[:held, :width] = out_part[k * held : (k + 1) * held]
        target[held:, :] = shared_low


def norm_back_kernel(rows, lengths, hidden, columns, *refs):
    middle_grads, refs = refs[:2], refs[2:]
    own_parts, near_parts = refs[0 : 2 * rows : 2], refs[1 : 2 * rows : 2]
    crossed, (out,) = refs[2 * rows : 2 * rows + rows // 2], refs[2 * rows + rows // 2 :]
    cross_parts = [part.at[place] for part in crossed for place in range(2)]
    gain = columns[:, 0:1]
    for row in range(rows):
        place = row_of(lengths, row, rows)
        unit, inverse = norm_columns(hidden[place].astype(F32))
        grad = (
            own_parts[row][...].astype(F32)
            + near_parts[row][0].astype(F32)
            + cross_parts[row][...].astype(F32)
        )
        half = rows // 2
        result = middle_grads[row // half][row % half] + norm_columns_back(
            grad, unit, inverse, gain
        )
        out[place] = result.astype(BF16)


def add_pieces_kernel(even, beside, *outs):
    for i, out in enumerate(outs):
        out[...] = (even[i].astype(F32) + beside[i].astype(F32)).astype(BF16)


def own_piece_kernel(first, second, fourth, sixth, norm_sums, out):
    size = first.shape[0]
    total = first[...].astype(F32) + second[...].astype(F32)
    total = total + fourth[...].astype(F32) + sixth[...].astype(F32)
    out[:size, :] = total.astype(BF16)
    width = norm_sums.shape[1]
    values = norm_sums[...]
    high = values.astype(BF16)
    rest = (values - high.astype(F32)).astype(BF16)
    out[size:, 384:] = jnp.zeros((16, LANES - 384), BF16)
    out[size:, :width] = jnp.concatenate([high.astype(F32), rest.astype(F32)]).astype(BF16)


def feed_sum_kernel(info, first, second, fourth, sixth, keep, send, rows):
    total = first[...].astype(F32) + second[...].astype(F32)
    rows[...] = total + fourth[...].astype(F32) + sixth[...].astype(F32)
    size = keep.shape[0]
    chip = info[0] >> 1
    keep[...] = rows[at_block(chip, size), :].astype(BF16)
    send[...] = rows[at_block(1 - chip, size), :].astype(BF16)


def feed_pair_kernel(info, kept, came, mine, other, rows):
    rows[...] = kept[...].astype(F32) + came[...].astype(F32)
    size = mine.shape[0]
    core = info[0] & 1
    mine[...] = rows[at_block(core, size), :].astype(BF16)
    other[...] = rows[at_block(1 - core, size), :].astype(BF16)


def unpack_kernel(info, *refs):
    evens, beside = refs[:4], refs[4]
    refs = refs[5:]
    if len(refs) > 12:
        mine, came, refs = refs[0], refs[1], refs[2:]
        up_grad, down_grad = refs[10:12]
        refs = refs[:10] + refs[12:]
        count = up_grad.shape[1]

        def write(up, down):
            up_grad[...] = up[:, :count].astype(F32)
            down_grad[...] = down[...].astype(F32).T[:count, :]

        pl.when(info[0] & 1 == 0)(lambda: write(mine, came))
        pl.when(info[0] & 1 == 1)(lambda: write(came, mine))
    weight_grad, bias_grad, out_grad, gain, shift, out_bias, down_bias, up_bias = refs[:8]
    norm_gain, norm_shift, whole, line = refs[8:]
    size = whole.shape[0] // 8
    width = weight_grad.shape[1]
    norms = [evens[0][size:, :].astype(F32) + beside[0, size:, :].astype(F32)]
    for i in range(4):
        whole[at_block(info[1] ^ (2 * i), size), :] = evens[i][:size, :].astype(F32)
        whole[at_block(info[1] ^ (2 * i + 1), size), :] = beside[i, :size, :].astype(F32)
        if i > 0:
            norms.append(evens[i][size:, :].astype(F32) + beside[i, size:, :].astype(F32))
    norms = (norms[0] + norms[1]) + (norms[2] + norms[3])
    norms = norms[:8] + norms[8:16]
    norm_gain[...] = norms[0:1, :width]
    norm_shift[...] = norms[1:2, :width]
    columns = weight_grad.shape[2]
    for c in range(3):
        turned = whole[c * columns : (c + 1) * columns, :].T
        weight_grad[c] = turned[:width, :]
        bias_grad[c : c + 1, :] = turned[width : width + 1, :]
    out_grad[...] = whole[3 * columns : 4 * columns, :width]
    for place, target in enumerate((gain, shift, out_bias, down_bias)):
        target[...] = whole[4 * columns + place : 4 * columns + place + 1, :width]
    block = up_bias.shape[0] // 8
    for j in range(8):
        line[:, j * block : (j + 1) * block] = whole[
            4 * columns + 4 + j : 4 * columns + 5 + j, :block
        ]
    up_bias[...] = line[0, :]


def swap(values, axis, bit):
    size = lax.axis_size(axis)
    return lax.ppermute(values, axis, [(i, i ^ bit) for i in range(size)])


def gather_four(own, *others):
    beside = swap(own, "tensor", 1)
    across = swap(own, "tensor", 2)
    return [own, beside, across, swap(after(across, *others), "tensor", 1)]


def spread_four(own, near, cross, beside, *others):
    across = swap(cross, "tensor", 2)
    return [own, beside, across, swap(after(across, *others), "tensor", 1)]


def add_low(*parts):
    total = parts[0].astype(F32)
    for part in parts[1:]:
        total = total + part.astype(F32)
    return total.astype(BF16)


def gather_feed_plain(up, down, core):
    pair = jnp.stack([up, down.T])
    pair = lax.all_gather(pair, "tensor", axis=1, tiled=True)
    pair = lax.all_gather(pair, "dp", axis=2, tiled=True)
    pair = pair.reshape(2, pair.shape[1], 8, -1).transpose(0, 2, 1, 3)
    pair = jnp.pad(pair, ((0, 0), (0, 0), (0, 0), (0, BLOCK - pair.shape[3])))
    pair = jnp.where(core == 0, pair, pair[::-1])
    feeds = []
    for half in (pair[0], pair[1]):
        feeds += [half[0], half[1], half[2], half[3], half[4::2], half[5::2]]
    return feeds


def scatter_feed_plain(kept, sent, core, hidden_count):
    grads = jnp.stack([kept, sent]).swapaxes(1, 2).reshape(2, 8, *kept.shape[2:])
    grads = jnp.where(core == 0, grads, grads[::-1]).astype(F32)
    grads = grads[:, :, :, : hidden_count * lax.axis_size("dp") // 8]
    grads = grads.transpose(0, 2, 1, 3).reshape(2, grads.shape[2], -1)
    grads = lax.psum_scatter(grads, "dp", scatter_dimension=2, tiled=True)
    grads = lax.psum_scatter(grads, "tensor", scatter_dimension=1, tiled=True)
    return grads[0], grads[1].T


def sum_pieces(even, beside, norm_sums):
    parts = call(
        add_pieces_kernel,
        (even, beside),
        [shape(even.shape[1:], BF16)] * 4,
        limit=4,
    )
    parts = [parts[0]] + [swap(parts[i], "dp", 2 * i) for i in (1, 2, 3)]
    norm_sums = norm_sums + swap(norm_sums, "tensor", 1)
    (own,) = call(
        own_piece_kernel,
        (*parts, norm_sums),
        [shape((even.shape[1] + 16, LANES), BF16)],
        limit=4,
    )
    back = [own] + [swap(own, "dp", e) for e in (2, 4, 6)]
    return back + [swap(jnp.stack(back), "dp", 1)], own


def sum_pieces_plain(even, odd, norm_sums):
    even, odd = (lax.psum(part.astype(F32), "dp").astype(BF16) for part in (even, odd))
    norm_sums = lax.psum(norm_sums, ("dp", "tensor"))
    high = norm_sums.astype(BF16)
    rest = (norm_sums - high.astype(F32)).astype(BF16)
    rows = jnp.concatenate([high, rest])
    rows = jnp.pad(rows, ((0, 0), (0, LANES - rows.shape[1])))
    even = jnp.concatenate([even, jnp.stack([rows] + [jnp.zeros_like(rows)] * 3)], axis=1)
    odd = jnp.concatenate([odd, jnp.zeros((4, *rows.shape), BF16)], axis=1)
    return [even[i] for i in range(4)] + [odd]


def shards(
    hidden_in,
    attn_gain,
    attn_shift,
    query_key_value_weight,
    query_key_value_bias,
    attention_output_weight,
    out_bias,
    ffn_gain,
    ffn_shift,
    up_projection_weight,
    up_projection_bias,
    down_projection_weight,
    down_bias,
    lengths,
    cotangent,
):
    chunks = lax.axis_size("tensor")
    ring = lax.axis_size("dp") == 8
    position = lax.axis_index("tensor")
    index = lax.axis_index("dp") if ring else jnp.int32(0)
    core = position & 1
    rows, chunk, width = hidden_in.shape
    full = chunk * chunks
    columns = query_key_value_weight.shape[2]
    heads = columns // HEAD_DIM
    hidden_count = up_projection_weight.shape[1]
    blocks = 8
    half = rows // 2

    info = jnp.stack([position, index]).astype(jnp.int32)
    lengths = lengths.astype(jnp.int32)
    inner_table, outer_table = (jnp.asarray(table) for table in rotary_constants(chunk, chunks))
    hidden = hidden_in.transpose(0, 2, 1)
    given = cotangent.transpose(0, 2, 1)

    if ring:
        inputs = (info, up_projection_weight, down_projection_weight)
        (pair,) = call(
            pair_kernel,
            inputs,
            [shape((columns, 2 * BLOCK), BF16)],
            scratch=[pltpu.VMEM(part.shape, part.dtype) for part in inputs[1:]]
            + [pltpu.SemaphoreType.DMA((2,))],
            in_specs=[smem()] + hbm(2),
            limit=4,
            tiles=20,
        )
        pair_across = swap(pair, "tensor", 2)
    inputs = (
        lengths,
        after(hidden, pair) if ring else hidden,
        attn_gain[None],
        attn_shift[None],
        attention_output_weight,
    )
    first, second = call(
        norm_kernel,
        inputs,
        [
            shape((half * width, chunk), BF16),
            shape((half * width + 2 * columns, chunk), BF16),
        ],
        scratch=[pltpu.VMEM(part.shape, part.dtype) for part in inputs[1:]]
        + [pltpu.VMEM((128, width), F32), pltpu.SemaphoreType.DMA((8,))],
        in_specs=[smem()] + hbm(4),
        limit=8,
        tiles=80,
    )
    inputs = (
        info,
        attn_gain[None],
        attn_shift[None],
        out_bias[None],
        ffn_gain[None],
        ffn_shift[None],
        down_bias[None],
        up_projection_bias[None],
        query_key_value_weight,
        query_key_value_bias,
    )
    weight, weight_turned, vectors, bias, up_bias, vector_rows = call(
        lambda *refs: prepare_kernel(heads, *refs),
        inputs,
        [
            shape((3 * columns, width), BF16),
            shape((width, 3 * columns), BF16),
            shape((width, 128), F32),
            shape((3 * columns, 128), F32),
            shape((BLOCK, 128), F32),
            shape((8, width), F32),
        ],
        scratch=[
            pltpu.VMEM((3 * columns, width), F32),
            pltpu.VMEM((128, BLOCK), F32),
        ]
        + [pltpu.VMEM(part.shape, part.dtype) for part in inputs[1:]]
        + [pltpu.SemaphoreType.DMA((9,))],
        in_specs=[smem()] + hbm(len(inputs) - 1),
        limit=8,
        tiles=60,
    )
    if ring:
        parts = [
            pair,
            swap(pair, "tensor", 1),
            pair_across,
            swap(after(pair_across, first), "tensor", 1),
        ]
        (own_feed,) = call(
            lambda *refs: assemble_kernel(chunks, *refs),
            (info, *parts),
            [shape((width, BLOCK), BF16)],
            scratch=[pltpu.VMEM((width, BLOCK), F32)],
            in_specs=[smem()] + vmem(chunks),
            limit=6,
            tiles=20,
        )
        came = [swap(own_feed, "dp", e) for e in (2, 4, 6)]
        beside = swap(own_feed, "dp", 1)
        second_beside = swap(came[0], "dp", 1)
        gathered = [
            gather_four(after(first, pair_across), own_feed, came[0], beside, weight)
        ]
    else:
        gathered = [gather_four(first)]

    kept = []
    mixed = []
    for g in range(2):
        if g == 1 and ring:
            gathered[1][0] = after(gathered[1][0], duo, beside, second_beside, mixed[0][3])
        inputs = (info, lengths, *gathered[g], weight, bias, inner_table, outer_table)
        outs = call(
            lambda *refs, g=g: attend_kernel(heads, chunks, chunk, g * half, half, *refs),
            inputs,
            [
                shape((half, 128, chunk), BF16),
                shape((half, 128, chunk), BF16),
                shape((half, 2, 128, chunk), BF16),
            ]
            + [shape((half, heads, HEAD_ROWS, full), BF16)] * 3
            + [
                shape((half, 8, full), F32),
                shape((half, 128, full), F32),
                shape((half, width, full), BF16),
            ],
            scratch=[
                pltpu.VMEM((heads, full, HEAD_ROWS), BF16),
                pltpu.VMEM((8, full), F32),
                pltpu.VMEM((3 * columns, full), F32),
                pltpu.VMEM((half, width, full), BF16),
                pltpu.SemaphoreType.DMA((half,)),
            ],
            in_specs=[smem(), smem()] + vmem(len(inputs) - 2),
            out_specs=vmem(8) + hbm(),
            limit=14,
            tiles=400,
        )
        kept.append(outs[3:])
        mixed.append(list(outs[:3]) + [swap(outs[1], "tensor", 1)])
        if g == 0:
            gathered.append(gather_four(after(second, gathered[0][2]), outs[0]))
            if ring:
                duo = jnp.stack([after(part, mixed[0][3], second_beside) for part in came[1:]])
                duo_beside = swap(duo, "dp", 1)
            else:
                feeds = gather_feed_plain(up_projection_weight, down_projection_weight, core)

    if ring:
        duo_beside = after(duo_beside, kept[1][0])
        feeds = [own_feed, beside, came[0], second_beside, duo, duo_beside]
        feeds += [swap(part, "tensor", 1) for part in feeds]
    feed_outs = []
    for g in range(2):
        last = g == 1
        others = (kept[1][0],) if g == 0 else (feed_outs[0][2],)
        ready = (mixed[1][3],) if g == 0 else (mixed_near,)
        inputs = (
            info,
            lengths,
            hidden,
            after(given, *ready),
            vectors,
            up_bias,
            *spread_four(*mixed[g], *others),
            *gathered[1],
        )
        if last:
            inputs = inputs + tuple(feed_outs[0][5:]) + (feed_outs[0][0],)
        else:
            inputs = inputs + tuple(feeds)
        carried = [
            shape((2, width, blocks * BLOCK), BF16),
            shape((2, width, blocks * BLOCK), F32),
            shape((chunks * 128, width), F32),
            shape((4, width, 128), F32),
            shape((blocks, BLOCK, 128), F32),
        ]
        sent = [
            shape((2, blocks // 2, width, BLOCK), BF16),
            shape((2, blocks // 2, width, BLOCK), BF16),
            shape((144, LANES), BF16),
            shape((2, 144, LANES), BF16),
            shape((144, LANES), BF16),
        ]
        tokens = half * chunk
        outs = call(
            lambda *refs, g=g, last=last: feed_kernel(
                chunks, blocks, g * half, half, last, *refs
            ),
            inputs,
            [
                shape((rows if last else half, width, chunk), BF16),
                shape((half, width, chunk), F32),
                shape((half, 128, chunk), BF16),
                shape((half, 128, chunk), BF16),
                shape((half, 2, 128, chunk), BF16),
            ]
            + (sent if last else carried),
            scratch=[
                pltpu.VMEM((chunks * 128, width), BF16),
                pltpu.VMEM((chunks * 128, tokens), BF16),
                pltpu.VMEM((width, tokens), F32),
                pltpu.VMEM((width, tokens), BF16),
                pltpu.VMEM((width, tokens), BF16),
                pltpu.VMEM((width, tokens), F32),
                pltpu.VMEM((width, tokens), F32),
                pltpu.VMEM((2, 2 * BLOCK, tokens), F32),
                pltpu.VMEM((2, 2 * BLOCK, tokens), F32),
                pltpu.VMEM((2, 2 * BLOCK, tokens), BF16),
                pltpu.VMEM((2, 2 * BLOCK, tokens), BF16),
                pltpu.VMEM((4, width, 128), F32),
                pltpu.VMEM((blocks, BLOCK, 128), F32),
                pltpu.VMEM((16, LANES), F32),
                pltpu.SemaphoreType.DMA((2, blocks)),
            ],
            in_specs=[smem(), smem()]
            + (
                vmem(len(inputs) - 2)
                if last
                else vmem(len(inputs) - 2 - len(feeds)) + [pl.BlockSpec(memory_space=pl.ANY)] * len(feeds)
            ),
            limit=22,
            tiles=500,
        )
        feed_outs.append(outs)
        if g == 0:
            mixed_near = swap(outs[3], "tensor", 1)
    hidden_out = feed_outs[1][0]
    middle_grads = [outs[1] for outs in feed_outs]
    feed_kept, feed_sent, out_own, out_near, out_cross = feed_outs[1][5:]

    mixed_grads = [spread_four(*feed_outs[0][2:5], mixed_near, feed_outs[1][2])]
    feed_sent, out_near = after((feed_sent, out_near), mixed_grads[0][3])
    out_came = swap(out_near, "tensor", 1)
    feed_came = swap(feed_sent, "tensor", 1)
    running = None
    reduced = []
    crossing = []
    for r in range(rows):
        last = r == rows - 1
        g = r // half
        inputs = (
            info,
            lengths,
            *mixed_grads[g],
            *kept[g],
            weight_turned,
            inner_table,
            outer_table,
        )
        if last and ring:
            running = after(running, *evens)
        if r > 0:
            inputs = inputs + (running,)
        if last:
            inputs = inputs + (out_own, out_came, out_across, weight, vector_rows)
        outs = call(
            lambda *refs, r=r, last=last: attend_back_kernel(
                heads, chunks, chunk, r, r % half, r == 0, last, *refs
            ),
            inputs,
            [
                shape((width, chunk), BF16),
                shape((2, width, chunk), BF16),
                shape((width, chunk), BF16),
            ]
            + (
                [shape((4, 64, LANES), BF16)] * 2 + [shape((8, width), F32)]
                if last
                else [shape((3 * columns, LANES + 128), F32)]
            ),
            scratch=[
                pltpu.VMEM((128, full), BF16),
                pltpu.VMEM((heads, HEAD_ROWS, full), BF16),
                pltpu.VMEM((heads, HEAD_ROWS, full), BF16),
                pltpu.VMEM((heads, full, HEAD_ROWS), BF16),
                pltpu.VMEM((heads, full, HEAD_ROWS), BF16),
                pltpu.VMEM((3, columns, full), F32),
                pltpu.VMEM((3 * columns, full), BF16),
                pltpu.VMEM((512, LANES), F32),
                pltpu.VMEM((width, full), BF16),
                pltpu.SemaphoreType.DMA(()),
            ],
            in_specs=[smem(), smem()] + vmem(9) + hbm() + vmem(len(inputs) - 12),
            limit=12,
            tiles=420,
        )
        if last:
            outs = list(outs)
            even, odd, norm_sums = outs[3:]
            if ring:
                odd = after(odd, reduced[5], *feed_came)
                beside_pieces = swap(odd, "dp", 1)
                norm_sums = norm_sums + swap(norm_sums, "tensor", 2)
                outs[1] = after(outs[1], beside_pieces, norm_sums)
        near = swap(outs[1], "tensor", 1)
        reduced += [outs[0], near, None]
        crossing.append((outs[2], near))
        if r >= 2:
            pair_sum = jnp.stack(
                [
                    add_low(after(cross, outs[0], out_across), near[1])
                    for cross, near in crossing[2 * r - 4 : 2 * r - 2]
                ]
            )
            reduced[3 * (2 * r - 3) + 2] = swap(pair_sum, "tensor", 2)
        if not last:
            running = outs[3]
        if r == 1:
            mixed_near = swap(feed_outs[1][3], "tensor", 1)
            mixed_grads.append(spread_four(*feed_outs[1][2:5], mixed_near, outs[0]))
        if r == 0:
            out_across = swap(
                add_low(after(out_cross, outs[0]), out_came[1]), "tensor", 2
            )
            if ring:
                feed_odd = add_low(after(feed_kept[1], outs[0]), feed_came[1])
                running = after(running, feed_odd)
                feed_odd = swap(feed_odd, "dp", 1)
        if r == 2 and ring:
            feed_kept = after(feed_kept, outs[0])
            evens = [
                add_low(feed_kept[0, i], feed_came[0, i], feed_odd[i]) for i in range(4)
            ]
            feed_came = [swap(evens[i], "dp", 2 * i) for i in (1, 2, 3)]
    own_parts = [part for place, part in enumerate(reduced) if place % 3 < 2]
    cross_parts = [part for part in reduced[2::3] if part is not None]
    inputs = (lengths, hidden, vectors, *middle_grads, *own_parts, *cross_parts)
    (grad_hidden,) = call(
        lambda *refs: norm_back_kernel(rows, *refs),
        inputs,
        [shape((rows, width, chunk), BF16)],
        in_specs=[smem()] + vmem(len(inputs) - 1),
        limit=12,
        tiles=120,
    )
    if ring:
        parts, own = sum_pieces(even, beside_pieces, norm_sums)
    else:
        parts = sum_pieces_plain(even, odd, norm_sums)
    if ring:
        keep, send = call(
            feed_sum_kernel,
            (info, after(evens[0], own), *feed_came),
            [shape((width // 2, BLOCK), BF16)] * 2,
            scratch=[pltpu.VMEM((width, BLOCK), F32)],
            in_specs=[smem()] + vmem(4),
            limit=4,
            tiles=20,
        )
        mine, other = call(
            feed_pair_kernel,
            (info, keep, after(swap(send, "tensor", 2), grad_hidden)),
            [shape((columns, BLOCK), BF16)] * 2,
            scratch=[pltpu.VMEM((width // 2, BLOCK), F32)],
            in_specs=[smem()] + vmem(2),
            limit=4,
            tiles=20,
        )
        feed_parts = (mine, swap(other, "tensor", 1))
    else:
        grad_up_weight, grad_down_weight = scatter_feed_plain(
            feed_kept, feed_sent, core, hidden_count
        )

    inputs = (info, *parts) + (feed_parts if ring else ())
    outs = [
        shape((3, width, columns), F32),
        shape((3, columns), F32),
        shape((columns, width), F32),
    ]
    outs += [shape((1, width), F32)] * 4
    outs += [shape(up_projection_bias.shape, F32)]
    outs += [shape((1, width), F32)] * 2
    if ring:
        outs += [shape((columns, hidden_count), F32), shape((hidden_count, columns), F32)]
    outs = call(
        unpack_kernel,
        inputs,
        outs,
        scratch=[
            pltpu.VMEM((512, LANES), F32),
            pltpu.VMEM((1, up_projection_bias.shape[0]), F32),
        ],
        in_specs=[smem()] + vmem(len(inputs) - 1),
        limit=8,
        tiles=60,
    )
    grad_qkv_weight, grad_qkv_bias, grad_out_weight = outs[:3]
    grad_ffn_gain, grad_ffn_shift, grad_out_bias, grad_down_bias, grad_up_bias = outs[3:8]
    grad_attn_gain, grad_attn_shift = outs[8:10]
    if ring:
        grad_up_weight, grad_down_weight = outs[10:]
    return (
        hidden_out.transpose(0, 2, 1),
        grad_hidden.transpose(0, 2, 1),
        grad_attn_gain[0],
        grad_attn_shift[0],
        grad_qkv_weight,
        grad_qkv_bias,
        grad_out_weight,
        grad_out_bias[0],
        grad_ffn_gain[0],
        grad_ffn_shift[0],
        grad_up_weight,
        grad_up_bias,
        grad_down_weight,
        grad_down_bias[0],
    )


def solution(mesh):
    return jax.shard_map(
        shards,
        mesh=mesh,
        in_specs=(
            P("dp", "tensor", None),
            P(),
            P(),
            P(None, None, "tensor"),
            P(None, "tensor"),
            P("tensor", None),
            P(),
            P(),
            P(),
            P("tensor", "dp"),
            P(),
            P("dp", "tensor"),
            P(),
            P("dp"),
            P("dp", "tensor", None),
        ),
        out_specs=(
            P("dp", "tensor", None),
            P("dp", "tensor", None),
            P(),
            P(),
            P(None, None, "tensor"),
            P(None, "tensor"),
            P("tensor", None),
            P(),
            P(),
            P(),
            P("tensor", "dp"),
            P(),
            P("dp", "tensor"),
            P(),
        ),
        check_vma=False,
    )
```

profile of v0, /device:TPU:0, one launch (start us, length us, event | category | flops | bytes accessed | tf_op | source)
XLA Modules:
  0.0 210.5 jit_solution(11210239981057318337)
XLA Ops:
  0.8 1.5 shard_map.272.refs_1_
  2.3 3.0 %collective-permute-start = (bf16[120,512]{1,0:T(8,128)(2,1)S(1)}, bf16[120,512]{1,0:T(8,128)(2,1)S(1)}, u32[]{:S(2)}, u32[]{:S(2)}) collective-permute-start(bf16[120,512]{1,0:T(8,128)(2,1)S(1)} %shard_map.272.refs_1_), channel_id=1, source_target_pairs={{0,2},{1,3},{2,0},{3,1},{4,6},{5,7},{6,4},{7,5},{8,10},{9,11},{10,... | collective-permute-start | bytes 368648 | tf_op jit(solution)/shard_map/ppermute | solution.py:875
  6.0 2.5 %shard_map.273 = (bf16[960,256]{1,0:T(8,128)(2,1)S(1)}, bf16[1200,256]{1,0:T(8,128)(2,1)S(1)}) custom-call(s32[4]{0:T(128)S(1)} %copy-done.4, bf16[4,480,256]{2,1,0:T(8,128)(2,1)} %bitcast.92, f32[1,480]{1,0:T(1,128)} %bitcast.105, f32[1,480]{1,0:T(1,128)} %bitcast.107, bf16[120,480]{1,0:T(8,128)(2,1)} %out_weight_in.1), custom_call_target="tpu_custom_call" | custom-call | flops 26843544 | tf_op jit(solution)/shard_map/pallas_call | solution.py:59
  8.6 1.7 collective-permute-start.1
  12.5 1.6 collective-permute-start.7
  14.1 1.6 collective-permute-start.6
  16.3 2.4 %shard_map.275 = (bf16[360,480]{1,0:T(8,128)(2,1)S(1)}, bf16[480,360]{1,0:T(8,128)(2,1)S(1)}, f32[480,128]{1,0:T(8,128)S(1)}, f32[360,128]{1,0:T(8,128)S(1)}, f3...) custom-call(s32[2]{0:T(128)S(1)} %pad_add_fusion.info.refs_0_, f32[1,480]{1,0:T(1,128)} %bitcast.106, f32[1,480]{1,0:T(1,128)} %bitcast.108, ...), custom_call_target="tpu_custom_call" | custom-call | flops 20132660 | tf_op jit(solution)/shard_map/pallas_call | solution.py:59
  18.6 2.1 %collective-permute-done.7.refs_15_ = bf16[480,256]{1,0:T(8,128)(2,1)S(1)} collective-permute-done((bf16[480,256]{1,0:T(8,128)(2,1)S(1)}, bf16[480,256]{1,0:T(8,128)(2,1)S(1)}, u32[]{:S(2)}, u32[]{:S(2)}) %collective-permute-start.7) | collective-permute-done | bytes 245792 | tf_op jit(solution)/shard_map/ppermute | solution.py:875
  22.5 3.6 %collective-permute-start.11 = (bf16[480,256]{1,0:T(8,128)(2,1)S(1)}, bf16[480,256]{1,0:T(8,128)(2,1)S(1)}, u32[]{:S(2)}, u32[]{:S(2)}) collective-permute-start(bf16[480,256]{1,0:T(8,128)(2,1)S(1)} %shard_map.274.refs_14_), channel_id=1, source_target_pairs={{0,24},{4,28},{8,16},{12,20},{16,8},{20,12},{24,0},{28,4},{1,25},{... | collective-permute-start | bytes 737288 | tf_op jit(solution)/shard_map/ppermute | solution.py:875
  27.6 10.2 %shard_map.276 = (bf16[2,128,256]{2,1,0:T(8,128)(2,1)S(1)}, bf16[2,128,256]{2,1,0:T(8,128)(2,1)S(1)}, bf16[2,2,128,256]{3,2,1,0:T(8,128)(2,1)S(1)}, bf16[2,5,32,...) custom-call(s32[2]{0:T(128)S(1)} %pad_add_fusion.info.refs_0_, ...), custom_call_target="tpu_custom_call" | custom-call | flops 134217728 | tf_op jit(solution)/shard_map/pallas_call | solution.py:59
  39.3 8.2 %collective-permute-done.4 = bf16[480,256]{1,0:T(8,128)(2,1)S(1)} collective-permute-done((bf16[480,256]{1,0:T(8,128)(2,1)S(1)}, bf16[480,256]{1,0:T(8,128)(2,1)S(1)}, u32[]{:S(2)}, u32[]{:S(2)}) %collective-permute-start.4) | collective-permute-done | bytes 245792 | tf_op jit(solution)/shard_map/ppermute | solution.py:875
  47.5 1.5 collective-permute-start.18
  50.3 12.4 %shard_map.277 = (bf16[2,128,256]{2,1,0:T(8,128)(2,1)S(1)}, bf16[2,128,256]{2,1,0:T(8,128)(2,1)S(1)}, bf16[2,2,128,256]{3,2,1,0:T(8,128)(2,1)S(1)}, bf16[2,5,32,...) custom-call(s32[2]{0:T(128)S(1)} %pad_add_fusion.info.refs_0_, ...), custom_call_target="tpu_custom_call" | custom-call | flops 134217728 | tf_op jit(solution)/shard_map/pallas_call | solution.py:59
  67.1 14.1 %shard_map.278 = (bf16[2,480,256]{2,1,0:T(8,128)(2,1)S(1)}, f32[2,480,256]{2,1,0:T(8,128)S(1)}, bf16[2,128,256]{2,1,0:T(8,128)(2,1)S(1)}, bf16[2,128,256]{2,1,0:...) custom-call(s32[2]{0:T(128)S(1)} %pad_add_fusion.info.refs_0_, ...), custom_call_target="tpu_custom_call" | custom-call | flops 167772160 | tf_op jit(solution)/shard_map/pallas_call | solution.py:59
  84.1 14.8 %shard_map.279 = (bf16[4,480,256]{2,1,0:T(8,128)(2,1)}, f32[2,480,256]{2,1,0:T(8,128)S(1)}, bf16[2,128,256]{2,1,0:T(8,128)(2,1)S(1)}, bf16[2,128,256]{2,1,0:T(8,...) custom-call(s32[2]{0:T(128)S(1)} %pad_add_fusion.info.refs_0_, ...), custom_call_target="tpu_custom_call" | custom-call | flops 167772160 | tf_op jit(solution)/shard_map/pallas_call | solution.py:59
  102.0 10.1 %shard_map.280 = (bf16[480,256]{1,0:T(8,128)(2,1)S(1)}, bf16[2,480,256]{2,1,0:T(8,128)(2,1)S(1)}, bf16[480,256]{1,0:T(8,128)(2,1)S(1)}, f32[360,640]{1,0:T(8,128)S(1)}) custom-call(s32[2]{0:T(128)S(1)} %pad_add_fusion.info.refs_0_, s32[4]{0:T(128)S(1)} %copy-done.5, bf16[2,128,256]{2,1,0:T(8,128)(2,1)S(1)} %get-tuple-element.156.refs_2_, ...), custom_call_target="tpu_custom_call" | custom-call | flops 140928608 | tf_op jit(solution)/shard_map/pallas_call | solution.py:59
  112.9 15.2 %shard_map.281 = (bf16[480,256]{1,0:T(8,128)(2,1)S(1)}, bf16[2,480,256]{2,1,0:T(8,128)(2,1)S(1)}, bf16[480,256]{1,0:T(8,128)(2,1)S(1)}, f32[360,640]{1,0:T(8,128)S(1)}) custom-call(s32[2]{0:T(128)S(1)} %pad_add_fusion.info.refs_0_, s32[4]{0:T(128)S(1)} %copy-done.5, bf16[2,128,256]{2,1,0:T(8,128)(2,1)S(1)} %get-tuple-element.156.refs_2_, ...), custom_call_target="tpu_custom_call" | custom-call | flops 140928608 | tf_op jit(solution)/shard_map/pallas_call | solution.py:59
  130.1 15.4 %shard_map.282 = (bf16[480,256]{1,0:T(8,128)(2,1)S(1)}, bf16[2,480,256]{2,1,0:T(8,128)(2,1)S(1)}, bf16[480,256]{1,0:T(8,128)(2,1)S(1)}, f32[360,640]{1,0:T(8,128)S(1)}) custom-call(s32[2]{0:T(128)S(1)} %pad_add_fusion.info.refs_0_, s32[4]{0:T(128)S(1)} %copy-done.5, bf16[2,128,256]{2,1,0:T(8,128)(2,1)S(1)} %get-tuple-element.168.refs_2_, ...), custom_call_target="tpu_custom_call" | custom-call | flops 140928608 | tf_op jit(solution)/shard_map/pallas_call | solution.py:59
  147.1 3.7 %collective-permute-start.43 = (bf16[480,256]{1,0:T(8,128)(2,1)S(1)}, bf16[480,256]{1,0:T(8,128)(2,1)S(1)}, u32[]{:S(2)}, u32[]{:S(2)}) collective-permute-start(bf16[480,256]{1,0:T(8,128)(2,1)S(1)} %get-tuple-element.244), channel_id=1, source_target_pairs={{0,24},{4,28},{8,16},{12,20},{16,8},{20,12},{24,0},{28,4},{1,25},{... | collective-permute-start | bytes 737288 | tf_op jit(solution)/shard_map/ppermute | solution.py:875
  151.6 15.6 %shard_map.283 = (bf16[480,256]{1,0:T(8,128)(2,1)S(1)}, bf16[2,480,256]{2,1,0:T(8,128)(2,1)S(1)}, bf16[480,256]{1,0:T(8,128)(2,1)S(1)}, bf16[4,64,512]{2,1,0:T(8...) custom-call(s32[2]{0:T(128)S(1)} %pad_add_fusion.info.refs_0_, s32[4]{0:T(128)S(1)} %copy-done.5, ...), custom_call_target="tpu_custom_call" | custom-call | flops 140928608 | tf_op jit(solution)/shard_map/pallas_call | solution.py:59
  167.3 5.3 %collective-permute-start.44 = (bf16[4,64,512]{2,1,0:T(8,128)(2,1)S(1)}, bf16[4,64,512]{2,1,0:T(8,128)(2,1)S(1)}, u32[]{:S(2)}, u32[]{:S(2)}) collective-permute-start(bf16[4,64,512]{2,1,0:T(8,128)(2,1)S(1)} %get-tuple-element.214), channel_id=1, source_target_pairs={{0,4},{4,0},{8,12},{12,8},{16,20},{20,16},{24,28},{28,24},{1,5},{5... | collective-permute-start | bytes 786440 | tf_op jit(solution)/shard_map/ppermute | solution.py:875
  173.8 2.5 %collective-permute-done.45 = f32[8,480]{1,0:T(8,128)S(1)} collective-permute-done((f32[8,480]{1,0:T(8,128)S(1)}, f32[8,480]{1,0:T(8,128)S(1)}, u32[]{:S(2)}, u32[]{:S(2)}) %collective-permute-start.45) | collective-permute-done | bytes 15392 | tf_op jit(solution)/shard_map/ppermute | solution.py:875
  176.4 2.7 %collective-permute-done.44.beside = bf16[4,64,512]{2,1,0:T(8,128)(2,1)S(1)} collective-permute-done((bf16[4,64,512]{2,1,0:T(8,128)(2,1)S(1)}, bf16[4,64,512]{2,1,0:T(8,128)(2,1)S(1)}, u32[]{:S(2)}, u32[]{:S(2)}) %collective-permute-start.44) | collective-permute-done | bytes 262176 | tf_op jit(solution)/shard_map/ppermute | solution.py:875
  179.8 2.6 %collective-permute-start.49 = (bf16[64,512]{1,0:T(8,128)(2,1)S(1)}, bf16[64,512]{1,0:T(8,128)(2,1)S(1)}, u32[]{:S(2)}, u32[]{:S(2)}) collective-permute-start(bf16[64,512]{1,0:T(8,128)(2,1)S(1)} %get-tuple-element.224), channel_id=1, source_target_pairs={{0,16},{4,20},{8,24},{12,28},{16,0},{20,4},{24,8},{28,12},{1,17},{... | collective-permute-start | bytes 196616 | tf_op jit(solution)/shard_map/ppermute | solution.py:875
  186.8 1.8 collective-permute-done.50.sixth
  188.6 2.1 collective-permute-start.54
  191.3 1.8 collective-permute-start.52
  193.1 2.8 %collective-permute-done.54.refs_3_ = bf16[80,512]{1,0:T(8,128)(2,1)S(1)} collective-permute-done((bf16[80,512]{1,0:T(8,128)(2,1)S(1)}, bf16[80,512]{1,0:T(8,128)(2,1)S(1)}, u32[]{:S(2)}, u32[]{:S(2)}) %collective-permute-start.54) | collective-permute-done | bytes 81952 | tf_op jit(solution)/shard_map/ppermute | solution.py:875
  195.9 2.8 %collective-permute-done.53.refs_2_ = bf16[80,512]{1,0:T(8,128)(2,1)S(1)} collective-permute-done((bf16[80,512]{1,0:T(8,128)(2,1)S(1)}, bf16[80,512]{1,0:T(8,128)(2,1)S(1)}, u32[]{:S(2)}, u32[]{:S(2)}) %collective-permute-start.53) | collective-permute-done | bytes 81952 | tf_op jit(solution)/shard_map/ppermute | solution.py:875
  198.7 1.8 collective-permute-start.55
  202.6 3.7 %shard_map.284 = bf16[4,480,256]{2,1,0:T(8,128)(2,1)} custom-call(s32[4]{0:T(128)S(1)} %copy-done.5, bf16[4,480,256]{2,1,0:T(8,128)(2,1)S(1)} %bitcast.95, f32[480,128]{1,0:T(8,128)S(1)} %get-tuple-element.146.refs_4_.refs_2_, f32[2,480,256]{2,1,0:T(8,128)S(1)} %get-tuple-element.165.refs_3_, f32[2,480,256]{2,1,0:T(8,128)S(1)} %get-tuple-element.166.refs_4_, ...), custom_call_target="tpu_custom_call" | custom-call | flops 40265320 | tf_op jit(solution)/shard_map/pallas_call | solution.py:59
  208.2 2.0 shard_map.289
  (132 shorter events, 36.0 us)
Async XLA Ops:
  8.6 13.4 %collective-permute-start.1 = (bf16[960,256]{1,0:T(8,128)(2,1)S(1)}, bf16[960,256]{1,0:T(8,128)(2,1)S(1)}, u32[]{:S(2)}, u32[]{:S(2)}) collective-permute-start(bf16[960,256]{1,0:T(8,128)(2,1)S(1)} %get-tuple-element.132.refs_2_), channel_id=1, source_target_pairs={{0,2},{1,3},{2,0},{3,1},{4,6},{5,7},{6,4},{7,5},{8,10},{9,11},{10,... | collective-permute-start | bytes 1474568 | tf_op jit(solution)/shard_map/ppermute | solution.py:875
  12.5 8.3 %collective-permute-start.7 = (bf16[480,256]{1,0:T(8,128)(2,1)S(1)}, bf16[480,256]{1,0:T(8,128)(2,1)S(1)}, u32[]{:S(2)}, u32[]{:S(2)}) collective-permute-start(bf16[480,256]{1,0:T(8,128)(2,1)S(1)} %shard_map.274.refs_14_), channel_id=1, source_target_pairs={{0,4},{4,0},{8,12},{12,8},{16,20},{20,16},{24,28},{28,24},{1,5},{5... | collective-permute-start | bytes 737288 | tf_op jit(solution)/shard_map/ppermute | solution.py:875
  14.1 7.9 %collective-permute-start.6 = (bf16[480,256]{1,0:T(8,128)(2,1)S(1)}, bf16[480,256]{1,0:T(8,128)(2,1)S(1)}, u32[]{:S(2)}, u32[]{:S(2)}) collective-permute-start(bf16[480,256]{1,0:T(8,128)(2,1)S(1)} %shard_map.274.refs_14_), channel_id=1, source_target_pairs={{0,8},{4,12},{8,0},{12,4},{16,24},{20,28},{24,16},{28,20},{1,9},{5... | collective-permute-start | bytes 737288 | tf_op jit(solution)/shard_map/ppermute | solution.py:875
  15.7 11.9 %collective-permute-start.5 = (bf16[960,256]{1,0:T(8,128)(2,1)S(1)}, bf16[960,256]{1,0:T(8,128)(2,1)S(1)}, u32[]{:S(2)}, u32[]{:S(2)}) collective-permute-start(bf16[960,256]{1,0:T(8,128)(2,1)S(1)} %get-tuple-element.132.refs_2_), channel_id=1, source_target_pairs={{0,1},{1,0},{2,3},{3,2},{4,5},{5,4},{6,7},{7,6},{8,9},{9,8},{10,11... | collective-permute-start | bytes 1474568 | tf_op jit(solution)/shard_map/ppermute | solution.py:875
  22.0 16.3 %collective-permute-start.13 = (bf16[1200,256]{1,0:T(8,128)(2,1)S(1)}, bf16[1200,256]{1,0:T(8,128)(2,1)S(1)}, u32[]{:S(2)}, u32[]{:S(2)}) collective-permute-start(bf16[1200,256]{1,0:T(8,128)(2,1)S(1)} %get-tuple-element.141.refs_2_.refs_10_), channel_id=1, source_target_pairs={{0,2},{1,3},{2,0},{3,1},{4,6},{5,7},{6,4},{7,5},{8,10},{9,11},{10,... | collective-permute-start | bytes 1843208 | tf_op jit(solution)/shard_map/ppermute | solution.py:875
  22.5 15.9 %collective-permute-start.11 = (bf16[480,256]{1,0:T(8,128)(2,1)S(1)}, bf16[480,256]{1,0:T(8,128)(2,1)S(1)}, u32[]{:S(2)}, u32[]{:S(2)}) collective-permute-start(bf16[480,256]{1,0:T(8,128)(2,1)S(1)} %shard_map.274.refs_14_), channel_id=1, source_target_pairs={{0,24},{4,28},{8,16},{12,20},{16,8},{20,12},{24,0},{28,4},{1,25},{... | collective-permute-start | bytes 737288 | tf_op jit(solution)/shard_map/ppermute | solution.py:875
  26.1 12.6 %collective-permute-start.10 = (bf16[480,256]{1,0:T(8,128)(2,1)S(1)}, bf16[480,256]{1,0:T(8,128)(2,1)S(1)}, u32[]{:S(2)}, u32[]{:S(2)}) collective-permute-start(bf16[480,256]{1,0:T(8,128)(2,1)S(1)} %collective-permute-done.6.refs_16_), channel_id=1, source_target_pairs={{0,4},{4,0},{8,12},{12,8},{16,20},{20,16},{24,28},{28,24},{1,5},{5... | collective-permute-start | bytes 737288 | tf_op jit(solution)/shard_map/ppermute | solution.py:875
  27.6 19.8 %collective-permute-start.4 = (bf16[480,256]{1,0:T(8,128)(2,1)S(1)}, bf16[480,256]{1,0:T(8,128)(2,1)S(1)}, u32[]{:S(2)}, u32[]{:S(2)}) collective-permute-start(bf16[480,256]{1,0:T(8,128)(2,1)S(1)} %shard_map.274.refs_14_), channel_id=1, source_target_pairs={{0,16},{4,20},{8,24},{12,28},{16,0},{20,4},{24,8},{28,12},{1,17},{... | collective-permute-start | bytes 737288 | tf_op jit(solution)/shard_map/ppermute | solution.py:875
  38.3 11.5 %collective-permute-start.12 = (bf16[1200,256]{1,0:T(8,128)(2,1)S(1)}, bf16[1200,256]{1,0:T(8,128)(2,1)S(1)}, u32[]{:S(2)}, u32[]{:S(2)}) collective-permute-start(bf16[1200,256]{1,0:T(8,128)(2,1)S(1)} %get-tuple-element.141.refs_2_.refs_10_), channel_id=1, source_target_pairs={{0,1},{1,0},{2,3},{3,2},{4,5},{5,4},{6,7},{7,6},{8,9},{9,8},{10,11... | collective-permute-start | bytes 1843208 | tf_op jit(solution)/shard_map/ppermute | solution.py:875
  38.4 11.6 %collective-permute-start.14 = (bf16[1200,256]{1,0:T(8,128)(2,1)S(1)}, bf16[1200,256]{1,0:T(8,128)(2,1)S(1)}, u32[]{:S(2)}, u32[]{:S(2)}) collective-permute-start(bf16[1200,256]{1,0:T(8,128)(2,1)S(1)} %collective-permute-done.13.refs_4_.refs_12_), channel_id=1, source_target_pairs={{0,1},{1,0},{2,3},{3,2},{4,5},{5,4},{6,7},{7,6},{8,9},{9,8},{10,11... | collective-permute-start | bytes 1843208 | tf_op jit(solution)/shard_map/ppermute | solution.py:875
  47.5 15.3 %collective-permute-start.18 = (bf16[2,480,256]{2,1,0:T(8,128)(2,1)S(1)}, bf16[2,480,256]{2,1,0:T(8,128)(2,1)S(1)}, u32[]{:S(2)}, u32[]{:S(2)}) collective-permute-start(bf16[2,480,256]{2,1,0:T(8,128)(2,1)S(1)} %pad_maximum_fusion.refs_18_), channel_id=1, source_target_pairs={{0,4},{4,0},{8,12},{12,8},{16,20},{20,16},{24,28},{28,24},{1,5},{5... | collective-permute-start | bytes 1474568 | tf_op jit(solution)/shard_map/ppermute | solution.py:875
  49.0 14.0 %collective-permute-start.19 = (bf16[480,256]{1,0:T(8,128)(2,1)S(1)}, bf16[480,256]{1,0:T(8,128)(2,1)S(1)}, u32[]{:S(2)}, u32[]{:S(2)}) collective-permute-start(bf16[480,256]{1,0:T(8,128)(2,1)S(1)} %shard_map.274.refs_14_), channel_id=1, source_target_pairs={{0,1},{1,0},{2,3},{3,2},{4,5},{5,4},{6,7},{7,6},{8,9},{9,8},{10,11... | collective-permute-start | bytes 737288 | tf_op jit(solution)/shard_map/ppermute | solution.py:875
  49.0 14.3 %collective-permute-start.16 = (bf16[2,2,128,256]{3,2,1,0:T(8,128)(2,1)S(1)}, bf16[2,2,128,256]{3,2,1,0:T(8,128)(2,1)S(1)}, u32[]{:S(2)}, u32[]{:S(2)}) collective-permute-start(bf16[2,2,128,256]{3,2,1,0:T(8,128)(2,1)S(1)} %get-tuple-element.148), channel_id=1, source_target_pairs={{0,2},{1,3},{2,0},{3,1},{4,6},{5,7},{6,4},{7,5},{8,10},{9,11},{10,... | collective-permute-start | bytes 786440 | tf_op jit(solution)/shard_map/ppermute | solution.py:875
  49.8 13.8 %collective-permute-start.20 = (bf16[480,256]{1,0:T(8,128)(2,1)S(1)}, bf16[480,256]{1,0:T(8,128)(2,1)S(1)}, u32[]{:S(2)}, u32[]{:S(2)}) collective-permute-start(bf16[480,256]{1,0:T(8,128)(2,1)S(1)} %collective-permute-done.7.refs_15_), channel_id=1, source_target_pairs={{0,1},{1,0},{2,3},{3,2},{4,5},{5,4},{6,7},{7,6},{8,9},{9,8},{10,11... | collective-permute-start | bytes 737288 | tf_op jit(solution)/shard_map/ppermute | solution.py:875
  50.0 13.8 %collective-permute-start.21 = (bf16[480,256]{1,0:T(8,128)(2,1)S(1)}, bf16[480,256]{1,0:T(8,128)(2,1)S(1)}, u32[]{:S(2)}, u32[]{:S(2)}) collective-permute-start(bf16[480,256]{1,0:T(8,128)(2,1)S(1)} %collective-permute-done.6.refs_16_), channel_id=1, source_target_pairs={{0,1},{1,0},{2,3},{3,2},{4,5},{5,4},{6,7},{7,6},{8,9},{9,8},{10,11... | collective-permute-start | bytes 737288 | tf_op jit(solution)/shard_map/ppermute | solution.py:875
  63.9 17.4 %collective-permute-start.26 = (bf16[2,2,128,256]{3,2,1,0:T(8,128)(2,1)S(1)}, bf16[2,2,128,256]{3,2,1,0:T(8,128)(2,1)S(1)}, u32[]{:S(2)}, u32[]{:S(2)}) collective-permute-start(bf16[2,2,128,256]{3,2,1,0:T(8,128)(2,1)S(1)} %get-tuple-element.155), channel_id=1, source_target_pairs={{0,2},{1,3},{2,0},{3,1},{4,6},{5,7},{6,4},{7,5},{8,10},{9,11},{10,... | collective-permute-start | bytes 786440 | tf_op jit(solution)/shard_map/ppermute | solution.py:875
  81.6 17.4 %collective-permute-start.28 = (bf16[2,2,128,256]{3,2,1,0:T(8,128)(2,1)S(1)}, bf16[2,2,128,256]{3,2,1,0:T(8,128)(2,1)S(1)}, u32[]{:S(2)}, u32[]{:S(2)}) collective-permute-start(bf16[2,2,128,256]{3,2,1,0:T(8,128)(2,1)S(1)} %get-tuple-element.167), channel_id=1, source_target_pairs={{0,2},{1,3},{2,0},{3,1},{4,6},{5,7},{6,4},{7,5},{8,10},{9,11},{10,... | collective-permute-start | bytes 786440 | tf_op jit(solution)/shard_map/ppermute | solution.py:875
  100.5 12.1 %collective-permute-start.31 = (bf16[2,4,480,256]{3,2,1,0:T(8,128)(2,1)S(1)}, bf16[2,4,480,256]{3,2,1,0:T(8,128)(2,1)S(1)}, u32[]{:S(2)}, u32[]{:S(2)}) collective-permute-start(bf16[2,4,480,256]{3,2,1,0:T(8,128)(2,1)S(1)} %get-tuple-element.184), channel_id=1, source_target_pairs={{0,1},{1,0},{2,3},{3,2},{4,5},{5,4},{6,7},{7,6},{8,9},{9,8},{10,11... | collective-permute-start | bytes 5898248 | tf_op jit(solution)/shard_map/ppermute | solution.py:875
  100.7 28.1 %collective-permute-start.33 = (bf16[2,128,256]{2,1,0:T(8,128)(2,1)S(1)}, bf16[2,128,256]{2,1,0:T(8,128)(2,1)S(1)}, u32[]{:S(2)}, u32[]{:S(2)}) collective-permute-start(bf16[2,128,256]{2,1,0:T(8,128)(2,1)S(1)} %get-tuple-element.188), channel_id=1, source_target_pairs={{0,1},{1,0},{2,3},{3,2},{4,5},{5,4},{6,7},{7,6},{8,9},{9,8},{10,11... | collective-permute-start | bytes 393224 | tf_op jit(solution)/shard_map/ppermute | solution.py:875
  101.0 27.1 %collective-permute-start.34 = (bf16[2,2,128,256]{3,2,1,0:T(8,128)(2,1)S(1)}, bf16[2,2,128,256]{3,2,1,0:T(8,128)(2,1)S(1)}, u32[]{:S(2)}, u32[]{:S(2)}) collective-permute-start(bf16[2,2,128,256]{3,2,1,0:T(8,128)(2,1)S(1)} %get-tuple-element.189), channel_id=1, source_target_pairs={{0,2},{1,3},{2,0},{3,1},{4,6},{5,7},{6,4},{7,5},{8,10},{9,11},{10,... | collective-permute-start | bytes 786440 | tf_op jit(solution)/shard_map/ppermute | solution.py:875
  101.9 26.4 %collective-permute-start.38 = (bf16[2,144,512]{2,1,0:T(8,128)(2,1)S(1)}, bf16[2,144,512]{2,1,0:T(8,128)(2,1)S(1)}, u32[]{:S(2)}, u32[]{:S(2)}) collective-permute-start(bf16[2,144,512]{2,1,0:T(8,128)(2,1)S(1)} %get-tuple-element.203), channel_id=1, source_target_pairs={{0,1},{1,0},{2,3},{3,2},{4,5},{5,4},{6,7},{7,6},{8,9},{9,8},{10,11... | collective-permute-start | bytes 884744 | tf_op jit(solution)/shard_map/ppermute | solution.py:875
  112.0 33.5 %collective-permute-start.30 = (bf16[2,480,256]{2,1,0:T(8,128)(2,1)S(1)}, bf16[2,480,256]{2,1,0:T(8,128)(2,1)S(1)}, u32[]{:S(2)}, u32[]{:S(2)}) collective-permute-start(bf16[2,480,256]{2,1,0:T(8,128)(2,1)S(1)} %get-tuple-element.178), channel_id=1, source_target_pairs={{0,1},{1,0},{2,3},{3,2},{4,5},{5,4},{6,7},{7,6},{8,9},{9,8},{10,11... | collective-permute-start | bytes 1474568 | tf_op jit(solution)/shard_map/ppermute | solution.py:875
  112.9 33.8 %collective-permute-start.37 = (bf16[4,480,256]{2,1,0:T(8,128)(2,1)S(1)}, bf16[4,480,256]{2,1,0:T(8,128)(2,1)S(1)}, u32[]{:S(2)}, u32[]{:S(2)}) collective-permute-start(bf16[4,480,256]{2,1,0:T(8,128)(2,1)S(1)} %fusion), channel_id=1, source_target_pairs={{0,4},{4,0},{8,12},{12,8},{16,20},{20,16},{24,28},{28,24},{1,5},{5... | collective-permute-start | bytes 2949128 | tf_op jit(solution)/shard_map/ppermute | solution.py:875
  128.3 17.3 %collective-permute-start.32 = (bf16[2,480,256]{2,1,0:T(8,128)(2,1)S(1)}, bf16[2,480,256]{2,1,0:T(8,128)(2,1)S(1)}, u32[]{:S(2)}, u32[]{:S(2)}) collective-permute-start(bf16[2,480,256]{2,1,0:T(8,128)(2,1)S(1)} %get-tuple-element.187), channel_id=1, source_target_pairs={{0,1},{1,0},{2,3},{3,2},{4,5},{5,4},{6,7},{7,6},{8,9},{9,8},{10,11... | collective-permute-start | bytes 1474568 | tf_op jit(solution)/shard_map/ppermute | solution.py:875
  128.8 16.7 %collective-permute-start.39 = (bf16[144,512]{1,0:T(8,128)(2,1)S(1)}, bf16[144,512]{1,0:T(8,128)(2,1)S(1)}, u32[]{:S(2)}, u32[]{:S(2)}) collective-permute-start(bf16[144,512]{1,0:T(8,128)(2,1)S(1)} %fusion.9), channel_id=1, source_target_pairs={{0,2},{1,3},{2,0},{3,1},{4,6},{5,7},{6,4},{7,5},{8,10},{9,11},{10,... | collective-permute-start | bytes 442376 | tf_op jit(solution)/shard_map/ppermute | solution.py:875
  145.7 21.5 %collective-permute-start.40 = (bf16[2,480,256]{2,1,0:T(8,128)(2,1)S(1)}, bf16[2,480,256]{2,1,0:T(8,128)(2,1)S(1)}, u32[]{:S(2)}, u32[]{:S(2)}) collective-permute-start(bf16[2,480,256]{2,1,0:T(8,128)(2,1)S(1)} %pad_maximum_fusion.1), channel_id=1, source_target_pairs={{0,2},{1,3},{2,0},{3,1},{4,6},{5,7},{6,4},{7,5},{8,10},{9,11},{10,... | collective-permute-start | bytes 1474568 | tf_op jit(solution)/shard_map/ppermute | solution.py:875
  147.1 20.1 %collective-permute-start.43 = (bf16[480,256]{1,0:T(8,128)(2,1)S(1)}, bf16[480,256]{1,0:T(8,128)(2,1)S(1)}, u32[]{:S(2)}, u32[]{:S(2)}) collective-permute-start(bf16[480,256]{1,0:T(8,128)(2,1)S(1)} %get-tuple-element.244), channel_id=1, source_target_pairs={{0,24},{4,28},{8,16},{12,20},{16,8},{20,12},{24,0},{28,4},{1,25},{... | collective-permute-start | bytes 737288 | tf_op jit(solution)/shard_map/ppermute | solution.py:875
  150.8 16.5 %collective-permute-start.42 = (bf16[480,256]{1,0:T(8,128)(2,1)S(1)}, bf16[480,256]{1,0:T(8,128)(2,1)S(1)}, u32[]{:S(2)}, u32[]{:S(2)}) collective-permute-start(bf16[480,256]{1,0:T(8,128)(2,1)S(1)} %get-tuple-element.245), channel_id=1, source_target_pairs={{0,16},{4,20},{8,24},{12,28},{16,0},{20,4},{24,8},{28,12},{1,17},{... | collective-permute-start | bytes 737288 | tf_op jit(solution)/shard_map/ppermute | solution.py:875
  150.8 16.5 %collective-permute-start.41 = (bf16[480,256]{1,0:T(8,128)(2,1)S(1)}, bf16[480,256]{1,0:T(8,128)(2,1)S(1)}, u32[]{:S(2)}, u32[]{:S(2)}) collective-permute-start(bf16[480,256]{1,0:T(8,128)(2,1)S(1)} %get-tuple-element.246), channel_id=1, source_target_pairs={{0,8},{4,12},{8,0},{12,4},{16,24},{20,28},{24,16},{28,20},{1,9},{5... | collective-permute-start | bytes 737288 | tf_op jit(solution)/shard_map/ppermute | solution.py:875
  167.3 11.8 %collective-permute-start.44 = (bf16[4,64,512]{2,1,0:T(8,128)(2,1)S(1)}, bf16[4,64,512]{2,1,0:T(8,128)(2,1)S(1)}, u32[]{:S(2)}, u32[]{:S(2)}) collective-permute-start(bf16[4,64,512]{2,1,0:T(8,128)(2,1)S(1)} %get-tuple-element.214), channel_id=1, source_target_pairs={{0,4},{4,0},{8,12},{12,8},{16,20},{20,16},{24,28},{28,24},{1,5},{5... | collective-permute-start | bytes 786440 | tf_op jit(solution)/shard_map/ppermute | solution.py:875
  183.8 18.8 %collective-permute-start.47 = (bf16[2,480,256]{2,1,0:T(8,128)(2,1)S(1)}, bf16[2,480,256]{2,1,0:T(8,128)(2,1)S(1)}, u32[]{:S(2)}, u32[]{:S(2)}) collective-permute-start(bf16[2,480,256]{2,1,0:T(8,128)(2,1)S(1)} %pad_maximum_fusion.2), channel_id=1, source_target_pairs={{0,2},{1,3},{2,0},{3,1},{4,6},{5,7},{6,4},{7,5},{8,10},{9,11},{10,... | collective-permute-start | bytes 1474568 | tf_op jit(solution)/shard_map/ppermute | solution.py:875
  198.7 9.3 %collective-permute-start.55 = (bf16[4,80,512]{2,1,0:T(8,128)(2,1)S(1)}, bf16[4,80,512]{2,1,0:T(8,128)(2,1)S(1)}, u32[]{:S(2)}, u32[]{:S(2)}) collective-permute-start(bf16[4,80,512]{2,1,0:T(8,128)(2,1)S(1)} %pad_maximum_fusion.3), channel_id=1, source_target_pairs={{0,4},{4,0},{8,12},{12,8},{16,20},{20,16},{24,28},{28,24},{1,5},{5... | collective-permute-start | bytes 983048 | tf_op jit(solution)/shard_map/ppermute | solution.py:875
  (33 other events, 240.5 us)
where the time goes:
time: 214 us; the launch traced here: 211 us
  Pallas kernels  122 us (57%)
  starting transfers between devices  50.9 us (24%)
  waiting for transfers between devices  33.7 us (16%)
    pallas_call x18, Pallas kernels, call(): pl.pallas_call(kernel, out_shape=outs, in_specs=in_specs, out_specs=out_s...  122 us
    ppermute x58, starting transfers between devices, swap(): return lax.ppermute(values, axis, [(i, i ^ bit) for i in range(size)])  50.9 us
    ppermute x58, waiting for transfers between devices, swap(): return lax.ppermute(values, axis, [(i, i ^ bit) for i in range(size)])  33.7 us
  transfers between devices with their start and end apart: 58, of which 21 were waited for; matrix products, arithmetic and copies ran while one was open for 1% of the time, Pallas kernels for 56%

commit v1 on v0

--- a/solution.py
+++ b/solution.py
@@ -343,7 +343,7 @@
                 query = jnp.where(
                     head_line == HEAD_DIM, -top, queries[r, h].astype(F32)
                 ).astype(BF16)
-                exponent = jnp.exp(product(key_rows[h, :count, :], query)).astype(BF16)
+                exponent = jnp.exp2(product(key_rows[h, :count, :], query) * LOG2E).astype(BF16)
                 blend = product(values[r, h, :, :count], exponent)
                 total = blend[HEAD_DIM : HEAD_DIM + 1, :]
                 logsum[r, pl.ds(h, 1), :] = top + jnp.log(total)
@@ -443,7 +443,7 @@
             grad_query = jnp.zeros((HEAD_ROWS, full), F32)
             for place in range(0, count, BLOCK):
                 at = slice(place, min(place + BLOCK, count))
-                probs = jnp.exp(product(key_rows[h, at, :], query_full[h])).astype(BF16)
+                probs = jnp.exp2(product(key_rows[h, at, :], query_full[h]) * LOG2E).astype(BF16)
                 grad_probs = product(value_rows[h, at, :], upstream_full[h]).astype(BF16)
                 grad_scores = probs * grad_probs
                 grads[2, own, at] = product(upstream_full[h], probs, NT)[:HEAD_DIM]

time: 214 us -> 209 us (0.977); the launches traced: 211 us -> 212 us
  Pallas kernels: 122 us -> 114 us
  starting transfers between devices: 50.9 us -> 58.1 us
    pallas_call x18, Pallas kernels: 122 us -> 114 us  [call(): pl.pallas_call(kernel, out_shape=outs, in_specs=in_specs, out_specs=out_s...]
    ppermute x58, starting transfers between devices: 50.9 us -> 58.1 us  [swap(): return lax.ppermute(values, axis, [(i, i ^ bit) for i in range(size)])]
  transfers between devices with their start and end apart: 58 -> 58, of which waited for: 21 -> 23; matrix products, arithmetic and copies ran while one was open for 1% -> 1% of each run, Pallas kernels for 56% -> 52%
where the time goes in v1:
time: 209 us; the launch traced here: 212 us
  Pallas kernels  114 us (55%)
  starting transfers between devices  58.1 us (28%)
  waiting for transfers between devices  35.3 us (17%)
    pallas_call x18, Pallas kernels, call(): pl.pallas_call(kernel, out_shape=outs, in_specs=in_specs, out_specs=out_s...  114 us
    ppermute x58, starting transfers between devices, swap(): return lax.ppermute(values, axis, [(i, i ^ bit) for i in range(size)])  58.1 us
    ppermute x58, waiting for transfers between devices, swap(): return lax.ppermute(values, axis, [(i, i ^ bit) for i in range(size)])  35.3 us
  transfers between devices with their start and end apart: 58, of which 23 were waited for; matrix products, arithmetic and copies ran while one was open for 1% of the time, Pallas kernels for 52%

profile of v1, /device:TPU:0, one launch (start us, length us, event | category | flops | bytes accessed | tf_op | source)
XLA Modules:
  0.0 211.6 jit_solution(11210239981057318337)
XLA Ops:
  0.8 1.5 shard_map.272.refs_1_
  2.3 3.0 %collective-permute-start = (bf16[120,512]{1,0:T(8,128)(2,1)S(1)}, bf16[120,512]{1,0:T(8,128)(2,1)S(1)}, u32[]{:S(2)}, u32[]{:S(2)}) collective-permute-start(bf16[120,512]{1,0:T(8,128)(2,1)S(1)} %shard_map.272.refs_1_), channel_id=1, source_target_pairs={{0,2},{1,3},{2,0},{3,1},{4,6},{5,7},{6,4},{7,5},{8,10},{9,11},{10,... | collective-permute-start | bytes 368648 | tf_op jit(solution)/shard_map/ppermute | solution.py:875
  6.0 2.5 %shard_map.273 = (bf16[960,256]{1,0:T(8,128)(2,1)S(1)}, bf16[1200,256]{1,0:T(8,128)(2,1)S(1)}) custom-call(s32[4]{0:T(128)S(1)} %copy-done.4, bf16[4,480,256]{2,1,0:T(8,128)(2,1)} %bitcast.92, f32[1,480]{1,0:T(1,128)} %bitcast.105, f32[1,480]{1,0:T(1,128)} %bitcast.107, bf16[120,480]{1,0:T(8,128)(2,1)} %out_weight_in.1), custom_call_target="tpu_custom_call" | custom-call | flops 26843544 | tf_op jit(solution)/shard_map/pallas_call | solution.py:59
  8.6 1.7 collective-permute-start.1
  12.5 1.6 collective-permute-start.7
  14.1 1.6 collective-permute-start.6
  16.3 2.4 %shard_map.275 = (bf16[360,480]{1,0:T(8,128)(2,1)S(1)}, bf16[480,360]{1,0:T(8,128)(2,1)S(1)}, f32[480,128]{1,0:T(8,128)S(1)}, f32[360,128]{1,0:T(8,128)S(1)}, f3...) custom-call(s32[2]{0:T(128)S(1)} %pad_add_fusion.info.refs_0_, f32[1,480]{1,0:T(1,128)} %bitcast.106, f32[1,480]{1,0:T(1,128)} %bitcast.108, ...), custom_call_target="tpu_custom_call" | custom-call | flops 20132660 | tf_op jit(solution)/shard_map/pallas_call | solution.py:59
  18.6 2.1 collective-permute-done.7.refs_15_
  22.5 3.6 %collective-permute-start.11 = (bf16[480,256]{1,0:T(8,128)(2,1)S(1)}, bf16[480,256]{1,0:T(8,128)(2,1)S(1)}, u32[]{:S(2)}, u32[]{:S(2)}) collective-permute-start(bf16[480,256]{1,0:T(8,128)(2,1)S(1)} %shard_map.274.refs_14_), channel_id=1, source_target_pairs={{0,24},{4,28},{8,16},{12,20},{16,8},{20,12},{24,0},{28,4},{1,25},{... | collective-permute-start | bytes 737288 | tf_op jit(solution)/shard_map/ppermute | solution.py:875
  27.6 10.2 %shard_map.276 = (bf16[2,128,256]{2,1,0:T(8,128)(2,1)S(1)}, bf16[2,128,256]{2,1,0:T(8,128)(2,1)S(1)}, bf16[2,2,128,256]{3,2,1,0:T(8,128)(2,1)S(1)}, bf16[2,5,32,...) custom-call(s32[2]{0:T(128)S(1)} %pad_add_fusion.info.refs_0_, ...), custom_call_target="tpu_custom_call" | custom-call | flops 134217728 | tf_op jit(solution)/shard_map/pallas_call | solution.py:59
  39.3 8.2 %collective-permute-done.4 = bf16[480,256]{1,0:T(8,128)(2,1)S(1)} collective-permute-done((bf16[480,256]{1,0:T(8,128)(2,1)S(1)}, bf16[480,256]{1,0:T(8,128)(2,1)S(1)}, u32[]{:S(2)}, u32[]{:S(2)}) %collective-permute-start.4) | collective-permute-done | bytes 245792 | tf_op jit(solution)/shard_map/ppermute | solution.py:875
  47.5 1.5 collective-permute-start.18
  50.3 10.3 %shard_map.277 = (bf16[2,128,256]{2,1,0:T(8,128)(2,1)S(1)}, bf16[2,128,256]{2,1,0:T(8,128)(2,1)S(1)}, bf16[2,2,128,256]{3,2,1,0:T(8,128)(2,1)S(1)}, bf16[2,5,32,...) custom-call(s32[2]{0:T(128)S(1)} %pad_add_fusion.info.refs_0_, ...), custom_call_target="tpu_custom_call" | custom-call | flops 134217728 | tf_op jit(solution)/shard_map/pallas_call | solution.py:59
  65.0 14.1 %shard_map.278 = (bf16[2,480,256]{2,1,0:T(8,128)(2,1)S(1)}, f32[2,480,256]{2,1,0:T(8,128)S(1)}, bf16[2,128,256]{2,1,0:T(8,128)(2,1)S(1)}, bf16[2,128,256]{2,1,0:...) custom-call(s32[2]{0:T(128)S(1)} %pad_add_fusion.info.refs_0_, ...), custom_call_target="tpu_custom_call" | custom-call | flops 167772160 | tf_op jit(solution)/shard_map/pallas_call | solution.py:59
  82.0 14.8 %shard_map.279 = (bf16[4,480,256]{2,1,0:T(8,128)(2,1)}, f32[2,480,256]{2,1,0:T(8,128)S(1)}, bf16[2,128,256]{2,1,0:T(8,128)(2,1)S(1)}, bf16[2,128,256]{2,1,0:T(8,...) custom-call(s32[2]{0:T(128)S(1)} %pad_add_fusion.info.refs_0_, ...), custom_call_target="tpu_custom_call" | custom-call | flops 167772160 | tf_op jit(solution)/shard_map/pallas_call | solution.py:59
  99.8 10.1 %shard_map.280 = (bf16[480,256]{1,0:T(8,128)(2,1)S(1)}, bf16[2,480,256]{2,1,0:T(8,128)(2,1)S(1)}, bf16[480,256]{1,0:T(8,128)(2,1)S(1)}, f32[360,640]{1,0:T(8,128)S(1)}) custom-call(s32[2]{0:T(128)S(1)} %pad_add_fusion.info.refs_0_, s32[4]{0:T(128)S(1)} %copy-done.5, bf16[2,128,256]{2,1,0:T(8,128)(2,1)S(1)} %get-tuple-element.156.refs_2_, ...), custom_call_target="tpu_custom_call" | custom-call | flops 140928608 | tf_op jit(solution)/shard_map/pallas_call | solution.py:59
  111.6 15.2 %shard_map.281 = (bf16[480,256]{1,0:T(8,128)(2,1)S(1)}, bf16[2,480,256]{2,1,0:T(8,128)(2,1)S(1)}, bf16[480,256]{1,0:T(8,128)(2,1)S(1)}, f32[360,640]{1,0:T(8,128)S(1)}) custom-call(s32[2]{0:T(128)S(1)} %pad_add_fusion.info.refs_0_, s32[4]{0:T(128)S(1)} %copy-done.5, bf16[2,128,256]{2,1,0:T(8,128)(2,1)S(1)} %get-tuple-element.156.refs_2_, ...), custom_call_target="tpu_custom_call" | custom-call | flops 140928608 | tf_op jit(solution)/shard_map/pallas_call | solution.py:59
  128.4 9.8 %shard_map.282 = (bf16[480,256]{1,0:T(8,128)(2,1)S(1)}, bf16[2,480,256]{2,1,0:T(8,128)(2,1)S(1)}, bf16[480,256]{1,0:T(8,128)(2,1)S(1)}, f32[360,640]{1,0:T(8,128)S(1)}) custom-call(s32[2]{0:T(128)S(1)} %pad_add_fusion.info.refs_0_, s32[4]{0:T(128)S(1)} %copy-done.5, bf16[2,128,256]{2,1,0:T(8,128)(2,1)S(1)} %get-tuple-element.168.refs_2_, ...), custom_call_target="tpu_custom_call" | custom-call | flops 140928608 | tf_op jit(solution)/shard_map/pallas_call | solution.py:59
  140.1 15.1 %collective-permute-start.43 = (bf16[480,256]{1,0:T(8,128)(2,1)S(1)}, bf16[480,256]{1,0:T(8,128)(2,1)S(1)}, u32[]{:S(2)}, u32[]{:S(2)}) collective-permute-start(bf16[480,256]{1,0:T(8,128)(2,1)S(1)} %get-tuple-element.244), channel_id=1, source_target_pairs={{0,24},{4,28},{8,16},{12,20},{16,8},{20,12},{24,0},{28,4},{1,25},{... | collective-permute-start | bytes 737288 | tf_op jit(solution)/shard_map/ppermute | solution.py:875
  155.9 15.6 %shard_map.283 = (bf16[480,256]{1,0:T(8,128)(2,1)S(1)}, bf16[2,480,256]{2,1,0:T(8,128)(2,1)S(1)}, bf16[480,256]{1,0:T(8,128)(2,1)S(1)}, bf16[4,64,512]{2,1,0:T(8...) custom-call(s32[2]{0:T(128)S(1)} %pad_add_fusion.info.refs_0_, s32[4]{0:T(128)S(1)} %copy-done.5, ...), custom_call_target="tpu_custom_call" | custom-call | flops 140928608 | tf_op jit(solution)/shard_map/pallas_call | solution.py:59
  171.8 2.0 collective-permute-start.44
  174.6 2.9 %collective-permute-done.45 = f32[8,480]{1,0:T(8,128)S(1)} collective-permute-done((f32[8,480]{1,0:T(8,128)S(1)}, f32[8,480]{1,0:T(8,128)S(1)}, u32[]{:S(2)}, u32[]{:S(2)}) %collective-permute-start.45) | collective-permute-done | bytes 15392 | tf_op jit(solution)/shard_map/ppermute | solution.py:875
  177.6 2.7 %collective-permute-done.44.beside = bf16[4,64,512]{2,1,0:T(8,128)(2,1)S(1)} collective-permute-done((bf16[4,64,512]{2,1,0:T(8,128)(2,1)S(1)}, bf16[4,64,512]{2,1,0:T(8,128)(2,1)S(1)}, u32[]{:S(2)}, u32[]{:S(2)}) %collective-permute-start.44) | collective-permute-done | bytes 262176 | tf_op jit(solution)/shard_map/ppermute | solution.py:875
  181.3 2.3 %collective-permute-start.49 = (bf16[64,512]{1,0:T(8,128)(2,1)S(1)}, bf16[64,512]{1,0:T(8,128)(2,1)S(1)}, u32[]{:S(2)}, u32[]{:S(2)}) collective-permute-start(bf16[64,512]{1,0:T(8,128)(2,1)S(1)} %get-tuple-element.224), channel_id=1, source_target_pairs={{0,16},{4,20},{8,24},{12,28},{16,0},{20,4},{24,8},{28,12},{1,17},{... | collective-permute-start | bytes 196616 | tf_op jit(solution)/shard_map/ppermute | solution.py:875
  187.1 2.8 %collective-permute-done.49.fourth = bf16[64,512]{1,0:T(8,128)(2,1)S(1)} collective-permute-done((bf16[64,512]{1,0:T(8,128)(2,1)S(1)}, bf16[64,512]{1,0:T(8,128)(2,1)S(1)}, u32[]{:S(2)}, u32[]{:S(2)}) %collective-permute-start.49) | collective-permute-done | bytes 65568 | tf_op jit(solution)/shard_map/ppermute | solution.py:875
  189.9 2.2 %collective-permute-start.54 = (bf16[80,512]{1,0:T(8,128)(2,1)S(1)}, bf16[80,512]{1,0:T(8,128)(2,1)S(1)}, u32[]{:S(2)}, u32[]{:S(2)}) collective-permute-start(bf16[80,512]{1,0:T(8,128)(2,1)S(1)} %shard_map.286.refs_0_), channel_id=1, source_target_pairs={{0,24},{4,28},{8,16},{12,20},{16,8},{20,12},{24,0},{28,4},{1,25},{... | collective-permute-start | bytes 245768 | tf_op jit(solution)/shard_map/ppermute | solution.py:875
  192.8 1.6 collective-permute-start.52
  194.4 2.7 %collective-permute-done.54.refs_3_ = bf16[80,512]{1,0:T(8,128)(2,1)S(1)} collective-permute-done((bf16[80,512]{1,0:T(8,128)(2,1)S(1)}, bf16[80,512]{1,0:T(8,128)(2,1)S(1)}, u32[]{:S(2)}, u32[]{:S(2)}) %collective-permute-start.54) | collective-permute-done | bytes 81952 | tf_op jit(solution)/shard_map/ppermute | solution.py:875
  197.1 2.8 %collective-permute-done.53.refs_2_ = bf16[80,512]{1,0:T(8,128)(2,1)S(1)} collective-permute-done((bf16[80,512]{1,0:T(8,128)(2,1)S(1)}, bf16[80,512]{1,0:T(8,128)(2,1)S(1)}, u32[]{:S(2)}, u32[]{:S(2)}) %collective-permute-start.53) | collective-permute-done | bytes 81952 | tf_op jit(solution)/shard_map/ppermute | solution.py:875
  199.9 1.8 collective-permute-start.55
  203.3 3.7 %shard_map.284 = bf16[4,480,256]{2,1,0:T(8,128)(2,1)} custom-call(s32[4]{0:T(128)S(1)} %copy-done.5, bf16[4,480,256]{2,1,0:T(8,128)(2,1)S(1)} %bitcast.95, f32[480,128]{1,0:T(8,128)S(1)} %get-tuple-element.146.refs_4_.refs_2_, f32[2,480,256]{2,1,0:T(8,128)S(1)} %get-tuple-element.165.refs_3_, f32[2,480,256]{2,1,0:T(8,128)S(1)} %get-tuple-element.166.refs_4_, ...), custom_call_target="tpu_custom_call" | custom-call | flops 40265320 | tf_op jit(solution)/shard_map/pallas_call | solution.py:59
  209.3 2.0 shard_map.289
  (132 shorter events, 35.7 us)
Async XLA Ops:
  8.6 13.4 %collective-permute-start.1 = (bf16[960,256]{1,0:T(8,128)(2,1)S(1)}, bf16[960,256]{1,0:T(8,128)(2,1)S(1)}, u32[]{:S(2)}, u32[]{:S(2)}) collective-permute-start(bf16[960,256]{1,0:T(8,128)(2,1)S(1)} %get-tuple-element.132.refs_2_), channel_id=1, source_target_pairs={{0,2},{1,3},{2,0},{3,1},{4,6},{5,7},{6,4},{7,5},{8,10},{9,11},{10,... | collective-permute-start | bytes 1474568 | tf_op jit(solution)/shard_map/ppermute | solution.py:875
  12.5 8.3 %collective-permute-start.7 = (bf16[480,256]{1,0:T(8,128)(2,1)S(1)}, bf16[480,256]{1,0:T(8,128)(2,1)S(1)}, u32[]{:S(2)}, u32[]{:S(2)}) collective-permute-start(bf16[480,256]{1,0:T(8,128)(2,1)S(1)} %shard_map.274.refs_14_), channel_id=1, source_target_pairs={{0,4},{4,0},{8,12},{12,8},{16,20},{20,16},{24,28},{28,24},{1,5},{5... | collective-permute-start | bytes 737288 | tf_op jit(solution)/shard_map/ppermute | solution.py:875
  15.7 11.9 %collective-permute-start.5 = (bf16[960,256]{1,0:T(8,128)(2,1)S(1)}, bf16[960,256]{1,0:T(8,128)(2,1)S(1)}, u32[]{:S(2)}, u32[]{:S(2)}) collective-permute-start(bf16[960,256]{1,0:T(8,128)(2,1)S(1)} %get-tuple-element.132.refs_2_), channel_id=1, source_target_pairs={{0,1},{1,0},{2,3},{3,2},{4,5},{5,4},{6,7},{7,6},{8,9},{9,8},{10,11... | collective-permute-start | bytes 1474568 | tf_op jit(solution)/shard_map/ppermute | solution.py:875
  22.0 16.3 %collective-permute-start.13 = (bf16[1200,256]{1,0:T(8,128)(2,1)S(1)}, bf16[1200,256]{1,0:T(8,128)(2,1)S(1)}, u32[]{:S(2)}, u32[]{:S(2)}) collective-permute-start(bf16[1200,256]{1,0:T(8,128)(2,1)S(1)} %get-tuple-element.141.refs_2_.refs_10_), channel_id=1, source_target_pairs={{0,2},{1,3},{2,0},{3,1},{4,6},{5,7},{6,4},{7,5},{8,10},{9,11},{10,... | collective-permute-start | bytes 1843208 | tf_op jit(solution)/shard_map/ppermute | solution.py:875
  22.5 15.9 %collective-permute-start.11 = (bf16[480,256]{1,0:T(8,128)(2,1)S(1)}, bf16[480,256]{1,0:T(8,128)(2,1)S(1)}, u32[]{:S(2)}, u32[]{:S(2)}) collective-permute-start(bf16[480,256]{1,0:T(8,128)(2,1)S(1)} %shard_map.274.refs_14_), channel_id=1, source_target_pairs={{0,24},{4,28},{8,16},{12,20},{16,8},{20,12},{24,0},{28,4},{1,25},{... | collective-permute-start | bytes 737288 | tf_op jit(solution)/shard_map/ppermute | solution.py:875
  26.1 12.6 %collective-permute-start.10 = (bf16[480,256]{1,0:T(8,128)(2,1)S(1)}, bf16[480,256]{1,0:T(8,128)(2,1)S(1)}, u32[]{:S(2)}, u32[]{:S(2)}) collective-permute-start(bf16[480,256]{1,0:T(8,128)(2,1)S(1)} %collective-permute-done.6.refs_16_), channel_id=1, source_target_pairs={{0,4},{4,0},{8,12},{12,8},{16,20},{20,16},{24,28},{28,24},{1,5},{5... | collective-permute-start | bytes 737288 | tf_op jit(solution)/shard_map/ppermute | solution.py:875
  27.6 19.8 %collective-permute-start.4 = (bf16[480,256]{1,0:T(8,128)(2,1)S(1)}, bf16[480,256]{1,0:T(8,128)(2,1)S(1)}, u32[]{:S(2)}, u32[]{:S(2)}) collective-permute-start(bf16[480,256]{1,0:T(8,128)(2,1)S(1)} %shard_map.274.refs_14_), channel_id=1, source_target_pairs={{0,16},{4,20},{8,24},{12,28},{16,0},{20,4},{24,8},{28,12},{1,17},{... | collective-permute-start | bytes 737288 | tf_op jit(solution)/shard_map/ppermute | solution.py:875
  38.3 11.5 %collective-permute-start.12 = (bf16[1200,256]{1,0:T(8,128)(2,1)S(1)}, bf16[1200,256]{1,0:T(8,128)(2,1)S(1)}, u32[]{:S(2)}, u32[]{:S(2)}) collective-permute-start(bf16[1200,256]{1,0:T(8,128)(2,1)S(1)} %get-tuple-element.141.refs_2_.refs_10_), channel_id=1, source_target_pairs={{0,1},{1,0},{2,3},{3,2},{4,5},{5,4},{6,7},{7,6},{8,9},{9,8},{10,11... | collective-permute-start | bytes 1843208 | tf_op jit(solution)/shard_map/ppermute | solution.py:875
  38.4 11.6 %collective-permute-start.14 = (bf16[1200,256]{1,0:T(8,128)(2,1)S(1)}, bf16[1200,256]{1,0:T(8,128)(2,1)S(1)}, u32[]{:S(2)}, u32[]{:S(2)}) collective-permute-start(bf16[1200,256]{1,0:T(8,128)(2,1)S(1)} %collective-permute-done.13.refs_4_.refs_12_), channel_id=1, source_target_pairs={{0,1},{1,0},{2,3},{3,2},{4,5},{5,4},{6,7},{7,6},{8,9},{9,8},{10,11... | collective-permute-start | bytes 1843208 | tf_op jit(solution)/shard_map/ppermute | solution.py:875
  47.5 13.1 %collective-permute-start.18 = (bf16[2,480,256]{2,1,0:T(8,128)(2,1)S(1)}, bf16[2,480,256]{2,1,0:T(8,128)(2,1)S(1)}, u32[]{:S(2)}, u32[]{:S(2)}) collective-permute-start(bf16[2,480,256]{2,1,0:T(8,128)(2,1)S(1)} %pad_maximum_fusion.refs_18_), channel_id=1, source_target_pairs={{0,4},{4,0},{8,12},{12,8},{16,20},{20,16},{24,28},{28,24},{1,5},{5... | collective-permute-start | bytes 1474568 | tf_op jit(solution)/shard_map/ppermute | solution.py:875
  49.0 11.9 %collective-permute-start.19 = (bf16[480,256]{1,0:T(8,128)(2,1)S(1)}, bf16[480,256]{1,0:T(8,128)(2,1)S(1)}, u32[]{:S(2)}, u32[]{:S(2)}) collective-permute-start(bf16[480,256]{1,0:T(8,128)(2,1)S(1)} %shard_map.274.refs_14_), channel_id=1, source_target_pairs={{0,1},{1,0},{2,3},{3,2},{4,5},{5,4},{6,7},{7,6},{8,9},{9,8},{10,11... | collective-permute-start | bytes 737288 | tf_op jit(solution)/shard_map/ppermute | solution.py:875
  49.0 12.2 %collective-permute-start.16 = (bf16[2,2,128,256]{3,2,1,0:T(8,128)(2,1)S(1)}, bf16[2,2,128,256]{3,2,1,0:T(8,128)(2,1)S(1)}, u32[]{:S(2)}, u32[]{:S(2)}) collective-permute-start(bf16[2,2,128,256]{3,2,1,0:T(8,128)(2,1)S(1)} %get-tuple-element.148), channel_id=1, source_target_pairs={{0,2},{1,3},{2,0},{3,1},{4,6},{5,7},{6,4},{7,5},{8,10},{9,11},{10,... | collective-permute-start | bytes 786440 | tf_op jit(solution)/shard_map/ppermute | solution.py:875
  49.8 11.6 %collective-permute-start.20 = (bf16[480,256]{1,0:T(8,128)(2,1)S(1)}, bf16[480,256]{1,0:T(8,128)(2,1)S(1)}, u32[]{:S(2)}, u32[]{:S(2)}) collective-permute-start(bf16[480,256]{1,0:T(8,128)(2,1)S(1)} %collective-permute-done.7.refs_15_), channel_id=1, source_target_pairs={{0,1},{1,0},{2,3},{3,2},{4,5},{5,4},{6,7},{7,6},{8,9},{9,8},{10,11... | collective-permute-start | bytes 737288 | tf_op jit(solution)/shard_map/ppermute | solution.py:875
  50.0 11.7 %collective-permute-start.21 = (bf16[480,256]{1,0:T(8,128)(2,1)S(1)}, bf16[480,256]{1,0:T(8,128)(2,1)S(1)}, u32[]{:S(2)}, u32[]{:S(2)}) collective-permute-start(bf16[480,256]{1,0:T(8,128)(2,1)S(1)} %collective-permute-done.6.refs_16_), channel_id=1, source_target_pairs={{0,1},{1,0},{2,3},{3,2},{4,5},{5,4},{6,7},{7,6},{8,9},{9,8},{10,11... | collective-permute-start | bytes 737288 | tf_op jit(solution)/shard_map/ppermute | solution.py:875
  61.7 17.4 %collective-permute-start.26 = (bf16[2,2,128,256]{3,2,1,0:T(8,128)(2,1)S(1)}, bf16[2,2,128,256]{3,2,1,0:T(8,128)(2,1)S(1)}, u32[]{:S(2)}, u32[]{:S(2)}) collective-permute-start(bf16[2,2,128,256]{3,2,1,0:T(8,128)(2,1)S(1)} %get-tuple-element.155), channel_id=1, source_target_pairs={{0,2},{1,3},{2,0},{3,1},{4,6},{5,7},{6,4},{7,5},{8,10},{9,11},{10,... | collective-permute-start | bytes 786440 | tf_op jit(solution)/shard_map/ppermute | solution.py:875
  79.4 17.4 %collective-permute-start.28 = (bf16[2,2,128,256]{3,2,1,0:T(8,128)(2,1)S(1)}, bf16[2,2,128,256]{3,2,1,0:T(8,128)(2,1)S(1)}, u32[]{:S(2)}, u32[]{:S(2)}) collective-permute-start(bf16[2,2,128,256]{3,2,1,0:T(8,128)(2,1)S(1)} %get-tuple-element.167), channel_id=1, source_target_pairs={{0,2},{1,3},{2,0},{3,1},{4,6},{5,7},{6,4},{7,5},{8,10},{9,11},{10,... | collective-permute-start | bytes 786440 | tf_op jit(solution)/shard_map/ppermute | solution.py:875
  98.4 12.1 %collective-permute-start.31 = (bf16[2,4,480,256]{3,2,1,0:T(8,128)(2,1)S(1)}, bf16[2,4,480,256]{3,2,1,0:T(8,128)(2,1)S(1)}, u32[]{:S(2)}, u32[]{:S(2)}) collective-permute-start(bf16[2,4,480,256]{3,2,1,0:T(8,128)(2,1)S(1)} %get-tuple-element.184), channel_id=1, source_target_pairs={{0,1},{1,0},{2,3},{3,2},{4,5},{5,4},{6,7},{7,6},{8,9},{9,8},{10,11... | collective-permute-start | bytes 5898248 | tf_op jit(solution)/shard_map/ppermute | solution.py:875
  98.5 28.9 %collective-permute-start.33 = (bf16[2,128,256]{2,1,0:T(8,128)(2,1)S(1)}, bf16[2,128,256]{2,1,0:T(8,128)(2,1)S(1)}, u32[]{:S(2)}, u32[]{:S(2)}) collective-permute-start(bf16[2,128,256]{2,1,0:T(8,128)(2,1)S(1)} %get-tuple-element.188), channel_id=1, source_target_pairs={{0,1},{1,0},{2,3},{3,2},{4,5},{5,4},{6,7},{7,6},{8,9},{9,8},{10,11... | collective-permute-start | bytes 393224 | tf_op jit(solution)/shard_map/ppermute | solution.py:875
  98.9 27.9 %collective-permute-start.34 = (bf16[2,2,128,256]{3,2,1,0:T(8,128)(2,1)S(1)}, bf16[2,2,128,256]{3,2,1,0:T(8,128)(2,1)S(1)}, u32[]{:S(2)}, u32[]{:S(2)}) collective-permute-start(bf16[2,2,128,256]{3,2,1,0:T(8,128)(2,1)S(1)} %get-tuple-element.189), channel_id=1, source_target_pairs={{0,2},{1,3},{2,0},{3,1},{4,6},{5,7},{6,4},{7,5},{8,10},{9,11},{10,... | collective-permute-start | bytes 786440 | tf_op jit(solution)/shard_map/ppermute | solution.py:875
  99.7 27.2 %collective-permute-start.38 = (bf16[2,144,512]{2,1,0:T(8,128)(2,1)S(1)}, bf16[2,144,512]{2,1,0:T(8,128)(2,1)S(1)}, u32[]{:S(2)}, u32[]{:S(2)}) collective-permute-start(bf16[2,144,512]{2,1,0:T(8,128)(2,1)S(1)} %get-tuple-element.203), channel_id=1, source_target_pairs={{0,1},{1,0},{2,3},{3,2},{4,5},{5,4},{6,7},{7,6},{8,9},{9,8},{10,11... | collective-permute-start | bytes 884744 | tf_op jit(solution)/shard_map/ppermute | solution.py:875
  109.9 28.4 %collective-permute-start.30 = (bf16[2,480,256]{2,1,0:T(8,128)(2,1)S(1)}, bf16[2,480,256]{2,1,0:T(8,128)(2,1)S(1)}, u32[]{:S(2)}, u32[]{:S(2)}) collective-permute-start(bf16[2,480,256]{2,1,0:T(8,128)(2,1)S(1)} %get-tuple-element.178), channel_id=1, source_target_pairs={{0,1},{1,0},{2,3},{3,2},{4,5},{5,4},{6,7},{7,6},{8,9},{9,8},{10,11... | collective-permute-start | bytes 1474568 | tf_op jit(solution)/shard_map/ppermute | solution.py:875
  110.7 29.0 %collective-permute-start.37 = (bf16[4,480,256]{2,1,0:T(8,128)(2,1)S(1)}, bf16[4,480,256]{2,1,0:T(8,128)(2,1)S(1)}, u32[]{:S(2)}, u32[]{:S(2)}) collective-permute-start(bf16[4,480,256]{2,1,0:T(8,128)(2,1)S(1)} %fusion), channel_id=1, source_target_pairs={{0,4},{4,0},{8,12},{12,8},{16,20},{20,16},{24,28},{28,24},{1,5},{5... | collective-permute-start | bytes 2949128 | tf_op jit(solution)/shard_map/ppermute | solution.py:875
  126.9 11.4 %collective-permute-start.32 = (bf16[2,480,256]{2,1,0:T(8,128)(2,1)S(1)}, bf16[2,480,256]{2,1,0:T(8,128)(2,1)S(1)}, u32[]{:S(2)}, u32[]{:S(2)}) collective-permute-start(bf16[2,480,256]{2,1,0:T(8,128)(2,1)S(1)} %get-tuple-element.187), channel_id=1, source_target_pairs={{0,1},{1,0},{2,3},{3,2},{4,5},{5,4},{6,7},{7,6},{8,9},{9,8},{10,11... | collective-permute-start | bytes 1474568 | tf_op jit(solution)/shard_map/ppermute | solution.py:875
  127.5 10.8 %collective-permute-start.39 = (bf16[144,512]{1,0:T(8,128)(2,1)S(1)}, bf16[144,512]{1,0:T(8,128)(2,1)S(1)}, u32[]{:S(2)}, u32[]{:S(2)}) collective-permute-start(bf16[144,512]{1,0:T(8,128)(2,1)S(1)} %fusion.9), channel_id=1, source_target_pairs={{0,2},{1,3},{2,0},{3,1},{4,6},{5,7},{6,4},{7,5},{8,10},{9,11},{10,... | collective-permute-start | bytes 442376 | tf_op jit(solution)/shard_map/ppermute | solution.py:875
  138.5 33.0 %collective-permute-start.40 = (bf16[2,480,256]{2,1,0:T(8,128)(2,1)S(1)}, bf16[2,480,256]{2,1,0:T(8,128)(2,1)S(1)}, u32[]{:S(2)}, u32[]{:S(2)}) collective-permute-start(bf16[2,480,256]{2,1,0:T(8,128)(2,1)S(1)} %pad_maximum_fusion.1), channel_id=1, source_target_pairs={{0,2},{1,3},{2,0},{3,1},{4,6},{5,7},{6,4},{7,5},{8,10},{9,11},{10,... | collective-permute-start | bytes 1474568 | tf_op jit(solution)/shard_map/ppermute | solution.py:875
  140.1 31.4 %collective-permute-start.43 = (bf16[480,256]{1,0:T(8,128)(2,1)S(1)}, bf16[480,256]{1,0:T(8,128)(2,1)S(1)}, u32[]{:S(2)}, u32[]{:S(2)}) collective-permute-start(bf16[480,256]{1,0:T(8,128)(2,1)S(1)} %get-tuple-element.244), channel_id=1, source_target_pairs={{0,24},{4,28},{8,16},{12,20},{16,8},{20,12},{24,0},{28,4},{1,25},{... | collective-permute-start | bytes 737288 | tf_op jit(solution)/shard_map/ppermute | solution.py:875
  155.2 16.6 %collective-permute-start.42 = (bf16[480,256]{1,0:T(8,128)(2,1)S(1)}, bf16[480,256]{1,0:T(8,128)(2,1)S(1)}, u32[]{:S(2)}, u32[]{:S(2)}) collective-permute-start(bf16[480,256]{1,0:T(8,128)(2,1)S(1)} %get-tuple-element.245), channel_id=1, source_target_pairs={{0,16},{4,20},{8,24},{12,28},{16,0},{20,4},{24,8},{28,12},{1,17},{... | collective-permute-start | bytes 737288 | tf_op jit(solution)/shard_map/ppermute | solution.py:875
  155.3 16.6 %collective-permute-start.41 = (bf16[480,256]{1,0:T(8,128)(2,1)S(1)}, bf16[480,256]{1,0:T(8,128)(2,1)S(1)}, u32[]{:S(2)}, u32[]{:S(2)}) collective-permute-start(bf16[480,256]{1,0:T(8,128)(2,1)S(1)} %get-tuple-element.246), channel_id=1, source_target_pairs={{0,8},{4,12},{8,0},{12,4},{16,24},{20,28},{24,16},{28,20},{1,9},{5... | collective-permute-start | bytes 737288 | tf_op jit(solution)/shard_map/ppermute | solution.py:875
  171.8 8.5 %collective-permute-start.44 = (bf16[4,64,512]{2,1,0:T(8,128)(2,1)S(1)}, bf16[4,64,512]{2,1,0:T(8,128)(2,1)S(1)}, u32[]{:S(2)}, u32[]{:S(2)}) collective-permute-start(bf16[4,64,512]{2,1,0:T(8,128)(2,1)S(1)} %get-tuple-element.214), channel_id=1, source_target_pairs={{0,4},{4,0},{8,12},{12,8},{16,20},{20,16},{24,28},{28,24},{1,5},{5... | collective-permute-start | bytes 786440 | tf_op jit(solution)/shard_map/ppermute | solution.py:875
  181.3 8.5 %collective-permute-start.49 = (bf16[64,512]{1,0:T(8,128)(2,1)S(1)}, bf16[64,512]{1,0:T(8,128)(2,1)S(1)}, u32[]{:S(2)}, u32[]{:S(2)}) collective-permute-start(bf16[64,512]{1,0:T(8,128)(2,1)S(1)} %get-tuple-element.224), channel_id=1, source_target_pairs={{0,16},{4,20},{8,24},{12,28},{16,0},{20,4},{24,8},{28,12},{1,17},{... | collective-permute-start | bytes 196616 | tf_op jit(solution)/shard_map/ppermute | solution.py:875
  185.0 18.3 %collective-permute-start.47 = (bf16[2,480,256]{2,1,0:T(8,128)(2,1)S(1)}, bf16[2,480,256]{2,1,0:T(8,128)(2,1)S(1)}, u32[]{:S(2)}, u32[]{:S(2)}) collective-permute-start(bf16[2,480,256]{2,1,0:T(8,128)(2,1)S(1)} %pad_maximum_fusion.2), channel_id=1, source_target_pairs={{0,2},{1,3},{2,0},{3,1},{4,6},{5,7},{6,4},{7,5},{8,10},{9,11},{10,... | collective-permute-start | bytes 1474568 | tf_op jit(solution)/shard_map/ppermute | solution.py:875
  199.9 9.1 %collective-permute-start.55 = (bf16[4,80,512]{2,1,0:T(8,128)(2,1)S(1)}, bf16[4,80,512]{2,1,0:T(8,128)(2,1)S(1)}, u32[]{:S(2)}, u32[]{:S(2)}) collective-permute-start(bf16[4,80,512]{2,1,0:T(8,128)(2,1)S(1)} %pad_maximum_fusion.3), channel_id=1, source_target_pairs={{0,4},{4,0},{8,12},{12,8},{16,20},{20,16},{24,28},{28,24},{1,5},{5... | collective-permute-start | bytes 983048 | tf_op jit(solution)/shard_map/ppermute | solution.py:875
  (33 other events, 235.9 us)
